TPU v7x, 128 devices: a whole 4x4x4 slice. The times are simulated.
128 devices in a mesh: region: 4 (over z_hi, core), tile: 32 (over x, y, z_lo).
Axes of the slice: x: 4, y: 4, z: 4 (z_hi: 2, z_lo: 2; z = z_hi * 2 + z_lo), core: 2. Of those that a mesh axis runs over, the one named last changes fastest.
Arguments:
- tokens: bfloat16 [512, 512, 512], P('tile', 'region'), may hold values from -6 to 6
- pore_mask: int32 [512, 512], P('tile', 'region'), may hold values 0 or 1
- solid_embed: float32 [512], replicated, may hold values from -4 to 4
- fine_query: bfloat16 [512, 512], replicated, as said below
- fine_key: bfloat16 [512, 512], replicated, as said below
- fine_value: bfloat16 [512, 512], replicated, may hold values from -0.25 to 0.25
- fine_out: bfloat16 [512, 512], replicated, may hold values from -0.25 to 0.25
- fine_scale: float32 [8], replicated, may hold values from 1 to 16
- coarse_query: bfloat16 [512, 512], replicated, as said below
- coarse_key: bfloat16 [512, 512], replicated, as said below
- coarse_value: bfloat16 [512, 512], replicated, may hold values from -0.25 to 0.25
- coarse_out: bfloat16 [512, 512], replicated, may hold values from -0.25 to 0.25
- coarse_scale: float32 [8], replicated, may hold values from 1 to 16
- mlp_in: bfloat16 [512, 2048], replicated, may hold values from -0.25 to 0.25
- mlp_out: bfloat16 [2048, 512], replicated, may hold values from -0.125 to 0.125
Outputs:
- updated: bfloat16 [512, 512, 512], P('tile', 'region')
Inputs may be any that keep to these rules, and one draw needn't show every extreme that they name: `fine_query`: entries of a projection of fan-in 512. `fine_key`: entries of a projection of fan-in 512. `coarse_query`: entries of a projection of fan-in 512. `coarse_key`: entries of a projection of fan-in 512.
All inputs are finite; a program needn't handle non-finite values. No bound on the sum of `pore_mask` on one device may be relied on, other than what follows from the above.
Results may differ from a plain program's by a relative error of at most 0.0081.
Values may be sent and summed in bfloat16 or wider, within the bound.
A program may use at most 128 MiB of HBM per device.

v0:
```python
import math

import jax
import jax.numpy as jnp
from jax import lax
from jax.sharding import PartitionSpec as P

HEADS = 8
HEAD_DIM = 64
RADIUS = 7
POOL = 8


epsilon = 1e-06


def with_halo(block, sides, width):
    for axis, dim in sides:
        count = lax.axis_size(axis)
        forward = [(i, i + 1) for i in range(count - 1)]
        forward.append((count - 1, 0))
        backward = [(target, source) for source, target in forward]
        low = lax.ppermute(
            lax.slice_in_dim(block, block.shape[dim] - width, None, axis=dim), axis, forward
        )
        high = lax.ppermute(lax.slice_in_dim(block, 0, width, axis=dim), axis, backward)
        block = jnp.concatenate([low, block, high], axis=dim)
    return block


def normalize_rows(values):
    return values * lax.rsqrt(jnp.mean(values * values, axis=-1, keepdims=True) + epsilon)


def head_normalize(projected):
    shape_in = projected.shape
    split = projected.reshape(shape_in[:-1] + (HEADS, HEAD_DIM))
    return normalize_rows(split).reshape(shape_in).astype(jnp.bfloat16)


def body(
    tokens,
    pore_mask,
    solid_embed,
    fine_query,
    fine_key,
    fine_value,
    fine_out,
    fine_scale,
    coarse_query,
    coarse_key,
    coarse_value,
    coarse_out,
    coarse_scale,
    mlp_in,
    mlp_out,
):
    tile_rows, tile_cols, model_width = tokens.shape
    stream = tokens.astype(jnp.float32) + pore_mask.astype(jnp.float32)[..., None] * solid_embed
    normed = normalize_rows(stream).astype(jnp.bfloat16)
    flat_rows = normed.reshape(-1, model_width)
    queries = head_normalize(jnp.dot(flat_rows, fine_query, preferred_element_type=jnp.float32))
    queries = queries.reshape(tile_rows, tile_cols, model_width)
    key_part = head_normalize(jnp.dot(flat_rows, fine_key, preferred_element_type=jnp.float32))
    value_part = jnp.dot(flat_rows, fine_value, preferred_element_type=jnp.float32).astype(
        jnp.bfloat16
    )
    local_pairs = jnp.concatenate([key_part, value_part], axis=-1).reshape(
        tile_rows, tile_cols, 2 * model_width
    )
    key_values = with_halo(local_pairs, (("region", 1), ("tile", 0)), RADIUS)
    block_cols = min(tile_cols, max(8, 512 // tile_rows))
    while tile_cols % block_cols:
        block_cols -= 1
    window_cols = block_cols + 2 * RADIUS
    window_rows = tile_rows + 2 * RADIUS
    query_index = jnp.arange(tile_rows * block_cols, dtype=jnp.int32)
    key_index = jnp.arange(window_rows * window_cols, dtype=jnp.int32)
    query_row = (query_index // block_cols)[:, None]
    query_col = (query_index % block_cols)[:, None]
    key_row = (key_index // window_cols)[None, :]
    key_col = (key_index % window_cols)[None, :]
    allowed = (
        (key_row >= query_row)
        & (key_row <= query_row + 2 * RADIUS)
        & (key_col >= query_col)
        & (key_col <= query_col + 2 * RADIUS)
    )
    fine_factor = (fine_scale / math.sqrt(HEAD_DIM))[:, None, None]

    def attend_block(block_index):
        offset = block_index * block_cols
        window = lax.dynamic_slice_in_dim(key_values, offset, window_cols, 1)
        key_rows = window[..., :model_width].reshape(-1, HEADS, HEAD_DIM)
        value_rows = window[..., model_width:].reshape(-1, HEADS, HEAD_DIM)
        query_rows = lax.dynamic_slice_in_dim(queries, offset, block_cols, 1).reshape(
            -1, HEADS, HEAD_DIM
        )
        scores = (
            jnp.einsum("qhd,khd->hqk", query_rows, key_rows, preferred_element_type=jnp.float32)
            * fine_factor
        )
        scores = jnp.where(allowed[None], scores, -jnp.inf)
        row_max = jnp.max(scores, axis=-1, keepdims=True)
        weights = jnp.exp(scores - row_max)
        weights_bf = (weights / jnp.sum(weights, axis=-1, keepdims=True)).astype(jnp.bfloat16)
        attended = jnp.einsum(
            "hqk,khd->qhd", weights_bf, value_rows, preferred_element_type=jnp.float32
        ).astype(jnp.bfloat16)
        return attended.reshape(tile_rows, block_cols, model_width)

    blocks = lax.map(attend_block, jnp.arange(tile_cols // block_cols, dtype=jnp.int32))
    fine_attn = jnp.transpose(blocks, (1, 0, 2, 3)).reshape(-1, model_width)
    pooled = jnp.mean(
        normed.reshape(tile_rows // POOL, POOL, tile_cols // POOL, POOL, model_width),
        axis=(1, 3),
        dtype=jnp.float32,
    )
    coarse_in = normalize_rows(pooled).astype(jnp.bfloat16).reshape(-1, model_width)
    coarse_count = coarse_in.shape[0]
    coarse_queries = head_normalize(
        jnp.dot(coarse_in, coarse_query, preferred_element_type=jnp.float32)
    ).reshape(-1, HEADS, HEAD_DIM)
    coarse_factor = (coarse_scale / math.sqrt(HEAD_DIM))[:, None, None]
    key_part = head_normalize(jnp.dot(coarse_in, coarse_key, preferred_element_type=jnp.float32))
    value_part = jnp.dot(coarse_in, coarse_value, preferred_element_type=jnp.float32).astype(
        jnp.bfloat16
    )
    run_max = jnp.full((HEADS, coarse_count), -jnp.inf, jnp.float32)
    run_sum = jnp.zeros((HEADS, coarse_count), jnp.float32)
    summed = jnp.zeros((HEADS, coarse_count, HEAD_DIM), jnp.float32)
    scores = (
        jnp.einsum(
            "qhd,khd->hqk",
            coarse_queries,
            lax.all_gather(key_part, ("region", "tile"), axis=0, tiled=True).reshape(
                -1, HEADS, HEAD_DIM
            ),
            preferred_element_type=jnp.float32,
        )
        * coarse_factor
    )
    new_max = jnp.max(scores, axis=-1)
    rescale = jnp.exp(run_max - new_max)
    weights = jnp.exp(scores - new_max[..., None])
    run_sum = run_sum * rescale + jnp.sum(weights, axis=-1)
    update = jnp.einsum(
        "hqk,khd->hqd",
        weights,
        lax.all_gather(value_part, ("region", "tile"), axis=0, tiled=True)
        .reshape(-1, HEADS, HEAD_DIM)
        .astype(jnp.float32),
        precision=lax.Precision.HIGHEST,
    )
    summed = summed * rescale[..., None] + update
    final_state = (new_max, run_sum, summed)
    run_max, run_sum, summed = final_state
    coarse_attn = (
        jnp.transpose(summed / run_sum[..., None], (1, 0, 2))
        .reshape(coarse_count, model_width)
        .astype(jnp.bfloat16)
    )
    block_shape = (tile_rows // POOL, POOL, tile_cols // POOL, POOL, model_width)
    feedback = jnp.dot(coarse_attn, coarse_out, preferred_element_type=jnp.float32).reshape(
        tile_rows // POOL, 1, tile_cols // POOL, 1, model_width
    )
    fine_proj = jnp.dot(fine_attn, fine_out, preferred_element_type=jnp.float32).reshape(
        block_shape
    )
    mixed = (stream.reshape(block_shape) + fine_proj + feedback).reshape(-1, model_width)
    normed_mixed = normalize_rows(mixed).astype(jnp.bfloat16)
    hidden = jax.nn.gelu(
        jnp.dot(normed_mixed, mlp_in, preferred_element_type=jnp.float32), approximate=False
    ).astype(jnp.bfloat16)
    updated = mixed + jnp.dot(hidden, mlp_out, preferred_element_type=jnp.float32)
    return updated.astype(jnp.bfloat16).reshape(tile_rows, tile_cols, model_width)


def solution(mesh):
    placed = (
        P("tile", "region", None),
        P("tile", "region"),
        P(),
        P(),
        P(),
        P(),
        P(),
        P(),
        P(),
        P(),
        P(),
        P(),
        P(),
        P(),
        P(),
    )
    return jax.shard_map(
        body, mesh=mesh, in_specs=placed, out_specs=P("tile", "region", None), check_vma=False
    )
```

profile of v0, /device:TPU:0, one launch (start us, length us, event | category | flops | bytes accessed | tf_op | source)
XLA Modules:
  0.0 758.3 jit_solution(18221745011963520088)
XLA Ops:
  26.3 6.5 copy.39
  50.4 20.4 %collective-permute-start.3 = (bf16[7,142,1024]{2,1,0:T(8,128)(2,1)}, bf16[7,142,1024]{2,1,0:T(8,128)(2,1)}, u32[]{:S(2)}, u32[]{:S(2)}) collective-permute-start(bf16[7,142,1024]{2,1,0:T(8,128)(2,1)} %get-tuple-element.114), channel_id=1, source_target_pairs={{1,0},{2,1},{3,2},{4,3},{5,4},{6,5},{7,6},{8,7},{9,8},{10,9},{11,1... | collective-permute-start | bytes 6107144 | tf_op jit(solution)/shard_map/ppermute | solution.py:26
  83.3 58.8 %collective-permute-done.2 = bf16[7,142,1024]{2,1,0:T(8,128)(2,1)} collective-permute-done((bf16[7,142,1024]{2,1,0:T(8,128)(2,1)}, bf16[7,142,1024]{2,1,0:T(8,128)(2,1)}, u32[]{:S(2)}, u32[]{:S(2)}) %collective-permute-start.2) | collective-permute-done | bytes 2035744 | tf_op jit(solution)/shard_map/ppermute | solution.py:23
  142.2 5.6 collective-permute-done.3
  147.7 8.3 %pad_maximum_fusion = bf16[30,142,1024]{2,1,0:T(8,128)(2,1)} fusion(bf16[7,142,1024]{2,1,0:T(8,128)(2,1)} %collective-permute-done.3, bf16[16,7,1024]{2,1,0:T(8,128)(2,1)S(1)} %collective-permute-done.1, bf16[16,128,1024]{2,1,0:T(8,128)(2,1)} %bitcast.116, bf16[16,7,1024]{2,1,0:T(8,128)(2,1)S(1)} %collective-permute-done, ...), kind=kLoop, calls=%fused_computation.42 | loop fusion | flops 43622400 | bytes 17448960 | tf_op jit(solution)/shard_map/concatenate | solution.py:27
  156.1 200.3 %while.11 = (s32[]{:T(128)}, bf16[4,16,32,512]{3,2,0,1:T(8,128)(2,1)}, s32[4]{0:T(128)S(1)}, bf16[30,142,1024]{2,1,0:T(8,128)(2,1)}, bf16[16,128,512]{2,1,0:T(8,...) while((s32[]{:T(128)}, ...), condition=%wide.region_6.7_spmd.clone, body=%wide.region_3.6_spmd.clone.sunk | while | flops 2226639616 | bytes 26629272 | solution.py:112
  161.9 5.1 constant_dynamic-slice_fusion.5
  171.5 9.4 %exponential_reduce_fusion.2 = f32[8,512]{1,0:T(8,128)S(1)} fusion(f32[8]{0:T(128)S(1)} %bitcast.135, pred[512,1380]{0,1:T(8,128)(4,1)} %compare_and_fusion.2, bf16[1380,8,64]{2,1,0:T(8,128)(2,1)} %reshape.288, bf16[512,8,64]{2,1,0:T(8,128)(2,1)S(1)} %copy-done.3), kind=kOutput, calls=%fused_computation.5.clone.1 | convolution fusion | flops 746128768 | bytes 2660384 | tf_op jit(solution)/shard_map/while/body/eval_jaxpr/sub | solution.py:105
  185.4 15.6 %fusion.154 = bf16[512,8,64]{0,2,1:T(8,128)(2,1)} fusion(f32[8,512]{1,0:T(8,128)S(1)} %exponential_reduce_fusion.2, f32[8]{0:T(128)S(1)} %bitcast.136, pred[512,1380]{0,1:T(8,128)(4,1)} %compare_and_fusion.2, bf16[1380,8,64]{2,1,0:T(8,128)(2,1)} %reshape.288, bf16[1380,8,64]{2,1,0:T(8,128)(2,1)} %reshape.290, bf16[512,8,64]{2,1,0:T(8,128)(2,1)S(1)} %copy-done.3), kind=kOutput, calls=%fused_computation.13.clone.1 | convolution fusion | flops 1475564928 | bytes 4597792 | tf_op jit(solution)/shard_map/while/body/eval_jaxpr/hqk,khd->qhd/dot_general | solution.py:107
  212.0 5.1 constant_dynamic-slice_fusion.5
  221.6 9.4 %exponential_reduce_fusion.2 = f32[8,512]{1,0:T(8,128)S(1)} fusion(f32[8]{0:T(128)S(1)} %bitcast.135, pred[512,1380]{0,1:T(8,128)(4,1)} %compare_and_fusion.2, bf16[1380,8,64]{2,1,0:T(8,128)(2,1)} %reshape.288, bf16[512,8,64]{2,1,0:T(8,128)(2,1)S(1)} %copy-done.3), kind=kOutput, calls=%fused_computation.5.clone.1 | convolution fusion | flops 746128768 | bytes 2660384 | tf_op jit(solution)/shard_map/while/body/eval_jaxpr/sub | solution.py:105
  235.6 15.7 %fusion.154 = bf16[512,8,64]{0,2,1:T(8,128)(2,1)} fusion(f32[8,512]{1,0:T(8,128)S(1)} %exponential_reduce_fusion.2, f32[8]{0:T(128)S(1)} %bitcast.136, pred[512,1380]{0,1:T(8,128)(4,1)} %compare_and_fusion.2, bf16[1380,8,64]{2,1,0:T(8,128)(2,1)} %reshape.288, bf16[1380,8,64]{2,1,0:T(8,128)(2,1)} %reshape.290, bf16[512,8,64]{2,1,0:T(8,128)(2,1)S(1)} %copy-done.3), kind=kOutput, calls=%fused_computation.13.clone.1 | convolution fusion | flops 1475564928 | bytes 4597792 | tf_op jit(solution)/shard_map/while/body/eval_jaxpr/hqk,khd->qhd/dot_general | solution.py:107
  271.7 9.4 %exponential_reduce_fusion.2 = f32[8,512]{1,0:T(8,128)S(1)} fusion(f32[8]{0:T(128)S(1)} %bitcast.135, pred[512,1380]{0,1:T(8,128)(4,1)} %compare_and_fusion.2, bf16[1380,8,64]{2,1,0:T(8,128)(2,1)} %reshape.288, bf16[512,8,64]{2,1,0:T(8,128)(2,1)S(1)} %copy-done.3), kind=kOutput, calls=%fused_computation.5.clone.1 | convolution fusion | flops 746128768 | bytes 2660384 | tf_op jit(solution)/shard_map/while/body/eval_jaxpr/sub | solution.py:105
  285.7 15.7 %fusion.154 = bf16[512,8,64]{0,2,1:T(8,128)(2,1)} fusion(f32[8,512]{1,0:T(8,128)S(1)} %exponential_reduce_fusion.2, f32[8]{0:T(128)S(1)} %bitcast.136, pred[512,1380]{0,1:T(8,128)(4,1)} %compare_and_fusion.2, bf16[1380,8,64]{2,1,0:T(8,128)(2,1)} %reshape.288, bf16[1380,8,64]{2,1,0:T(8,128)(2,1)} %reshape.290, bf16[512,8,64]{2,1,0:T(8,128)(2,1)S(1)} %copy-done.3), kind=kOutput, calls=%fused_computation.13.clone.1 | convolution fusion | flops 1475564928 | bytes 4597792 | tf_op jit(solution)/shard_map/while/body/eval_jaxpr/hqk,khd->qhd/dot_general | solution.py:107
  321.7 9.4 %exponential_reduce_fusion.2 = f32[8,512]{1,0:T(8,128)S(1)} fusion(f32[8]{0:T(128)S(1)} %bitcast.135, pred[512,1380]{0,1:T(8,128)(4,1)} %compare_and_fusion.2, bf16[1380,8,64]{2,1,0:T(8,128)(2,1)} %reshape.288, bf16[512,8,64]{2,1,0:T(8,128)(2,1)S(1)} %copy-done.3), kind=kOutput, calls=%fused_computation.5.clone.1 | convolution fusion | flops 746128768 | bytes 2660384 | tf_op jit(solution)/shard_map/while/body/eval_jaxpr/sub | solution.py:105
  335.6 15.6 %fusion.154 = bf16[512,8,64]{0,2,1:T(8,128)(2,1)} fusion(f32[8,512]{1,0:T(8,128)S(1)} %exponential_reduce_fusion.2, f32[8]{0:T(128)S(1)} %bitcast.136, pred[512,1380]{0,1:T(8,128)(4,1)} %compare_and_fusion.2, bf16[1380,8,64]{2,1,0:T(8,128)(2,1)} %reshape.288, bf16[1380,8,64]{2,1,0:T(8,128)(2,1)} %reshape.290, bf16[512,8,64]{2,1,0:T(8,128)(2,1)S(1)} %copy-done.3), kind=kOutput, calls=%fused_computation.13.clone.1 | convolution fusion | flops 1475564928 | bytes 4597792 | tf_op jit(solution)/shard_map/while/body/eval_jaxpr/hqk,khd->qhd/dot_general | solution.py:107
  356.4 20.5 %all-gather.3.cloned.1.call-done = bf16[4096,512]{1,0:T(8,128)(2,1)} async-done(((bf16[32,512]{1,0:T(8,128)(2,1)}), bf16[4096,512]{1,0:T(8,128)(2,1)}) %all-gather.3.cloned.1.call-update) | async-done | bytes 4194320 | tf_op jit(solution)/shard_map/all_gather | solution.py:136
  376.9 6.4 copy.35
  389.0 293.7 %all-gather.5.cloned.1.call-done = bf16[4096,512]{1,0:T(8,128)(2,1)} async-done(((bf16[32,512]{1,0:T(8,128)(2,1)}), bf16[4096,512]{1,0:T(8,128)(2,1)}) %all-gather.5.cloned.1.call-update) | async-done | bytes 4194320 | tf_op jit(solution)/shard_map/all_gather | solution.py:150
  682.7 6.4 copy.36
  689.1 7.3 fusion.57
  696.8 6.3 multiply_reduce_fusion
  705.8 39.3 %fusion.141 = bf16[2048,2048]{1,0:T(8,128)(2,1)S(1)} fusion(bf16[2048,512]{1,0:T(8,128)(2,1)S(1)} %fusion.45, bf16[512,2048]{1,0:T(8,128)(2,1)S(1)} %copy-done), kind=kOutput, calls=%fused_computation.26.clone.clone.clone.clone.1 | convolution fusion | flops 4567597056 | bytes 12582912 | tf_op jit(solution)/shard_map/dot_general | solution.py:173
  745.1 6.0 fusion.46
  (138 shorter events, 145.4 us)
Async XLA Ops:
  6.5 699.2 %copy-start = (bf16[512,2048]{1,0:T(8,128)(2,1)S(1)}, bf16[512,2048]{1,0:T(8,128)(2,1)}, u32[]{:S(2)}) copy-start(bf16[512,2048]{1,0:T(8,128)(2,1)} %param.30) | copy-start | bytes 6291460
  6.5 370.4 %all-gather.3.cloned.1.call-start = ((), (), s32[]{:S(2)}) async-start(), calls=%async_computation | async-start | bytes 4227072 | tf_op jit(solution)/shard_map/all_gather | solution.py:136
  11.5 7.0 copy-start.11
  18.4 664.3 %all-gather.5.cloned.1.call-start = ((), (), s32[]{:S(2)}) async-start(), calls=%async_computation.1 | async-start | bytes 4227072 | tf_op jit(solution)/shard_map/all_gather | solution.py:150
  18.7 3.1 copy-start.6
  26.3 11.8 %copy-start.9 = (bf16[512,512]{1,0:T(8,128)(2,1)S(1)}, bf16[512,512]{1,0:T(8,128)(2,1)}, u32[]{:S(2)}) copy-start(bf16[512,512]{1,0:T(8,128)(2,1)} %param.27) | copy-start | bytes 1572868
  34.6 10.7 %collective-permute-start = (bf16[16,7,1024]{2,1,0:T(8,128)(2,1)}, bf16[16,7,1024]{2,1,0:T(8,128)(2,1)S(1)}, u32[]{:S(2)}, u32[]{:S(2)}) collective-permute-start(bf16[16,7,1024]{2,1,0:T(8,128)(2,1)} %get-tuple-element.115), channel_id=1, source_target_pairs={{0,32},{32,64},{64,96},{96,0},{1,33},{33,65},{65,97},{97,1},{2,34}... | collective-permute-start | bytes 688136 | tf_op jit(solution)/shard_map/ppermute | solution.py:23
  34.6 10.7 %collective-permute-start.1 = (bf16[16,7,1024]{2,1,0:T(8,128)(2,1)S(1)}, bf16[16,7,1024]{2,1,0:T(8,128)(2,1)S(1)}, u32[]{:S(2)}, u32[]{:S(2)}) collective-permute-start(bf16[16,7,1024]{2,1,0:T(8,128)(2,1)S(1)} %get-tuple-element.116), channel_id=1, source_target_pairs={{32,0},{64,32},{96,64},{0,96},{33,1},{65,33},{97,65},{1,97},{34,2}... | collective-permute-start | bytes 688136 | tf_op jit(solution)/shard_map/ppermute | solution.py:26
  40.2 5.1 copy-start.1
  48.6 93.6 %collective-permute-start.2 = (bf16[7,142,1024]{2,1,0:T(8,128)(2,1)}, bf16[7,142,1024]{2,1,0:T(8,128)(2,1)}, u32[]{:S(2)}, u32[]{:S(2)}) collective-permute-start(bf16[7,142,1024]{2,1,0:T(8,128)(2,1)} %get-tuple-element.113), channel_id=1, source_target_pairs={{0,1},{1,2},{2,3},{3,4},{4,5},{5,6},{6,7},{7,8},{8,9},{9,10},{10,1... | collective-permute-start | bytes 6107144 | tf_op jit(solution)/shard_map/ppermute | solution.py:23
  50.4 97.3 %collective-permute-start.3 = (bf16[7,142,1024]{2,1,0:T(8,128)(2,1)}, bf16[7,142,1024]{2,1,0:T(8,128)(2,1)}, u32[]{:S(2)}, u32[]{:S(2)}) collective-permute-start(bf16[7,142,1024]{2,1,0:T(8,128)(2,1)} %get-tuple-element.114), channel_id=1, source_target_pairs={{1,0},{2,1},{3,2},{4,3},{5,4},{6,5},{7,6},{8,7},{9,8},{10,9},{11,1... | collective-permute-start | bytes 6107144 | tf_op jit(solution)/shard_map/ppermute | solution.py:26
  74.8 6.3 copy-start.15
  74.9 6.3 copy-start.16
  161.9 9.6 %copy-start.3 = (bf16[512,8,64]{2,1,0:T(8,128)(2,1)S(1)}, bf16[512,8,64]{2,1,0:T(8,128)(2,1)}, u32[]{:S(2)}) copy-start(bf16[512,8,64]{2,1,0:T(8,128)(2,1)} %reshape.289) | copy-start | bytes 1572868 | tf_op jit(solution)/shard_map/while
  212.0 9.6 %copy-start.3 = (bf16[512,8,64]{2,1,0:T(8,128)(2,1)S(1)}, bf16[512,8,64]{2,1,0:T(8,128)(2,1)}, u32[]{:S(2)}) copy-start(bf16[512,8,64]{2,1,0:T(8,128)(2,1)} %reshape.289) | copy-start | bytes 1572868 | tf_op jit(solution)/shard_map/while
  262.2 9.6 %copy-start.3 = (bf16[512,8,64]{2,1,0:T(8,128)(2,1)S(1)}, bf16[512,8,64]{2,1,0:T(8,128)(2,1)}, u32[]{:S(2)}) copy-start(bf16[512,8,64]{2,1,0:T(8,128)(2,1)} %reshape.289) | copy-start | bytes 1572868 | tf_op jit(solution)/shard_map/while
  312.3 9.4 %copy-start.3 = (bf16[512,8,64]{2,1,0:T(8,128)(2,1)S(1)}, bf16[512,8,64]{2,1,0:T(8,128)(2,1)}, u32[]{:S(2)}) copy-start(bf16[512,8,64]{2,1,0:T(8,128)(2,1)} %reshape.289) | copy-start | bytes 1572868 | tf_op jit(solution)/shard_map/while
  356.4 26.9 %copy-start.7 = (f32[32,8,64]{2,0,1:T(8,128)S(1)}, f32[32,8,64]{2,0,1:T(8,128)}, u32[]{:S(2)}) copy-start(f32[32,8,64]{2,0,1:T(8,128)} %get-tuple-element.126) | copy-start | bytes 196612
  356.4 26.9 %copy-start.12 = (f32[32,8]{0,1:T(8,128)S(1)}, f32[32,8]{0,1:T(8,128)}, u32[]{:S(2)}) copy-start(f32[32,8]{0,1:T(8,128)} %add_rsqrt_fusion.5) | copy-start | bytes 3076
  356.4 26.9 %copy-start.13 = (f32[8]{0:T(128)S(1)}, f32[8]{0:T(128)}, u32[]{:S(2)}) copy-start(f32[8]{0:T(128)} %broadcast_multiply_fusion) | copy-start | bytes 100
  689.1 7.5 copy-start.10
  689.1 7.6 %copy-start.8 = (bf16[512,512]{1,0:T(8,128)(2,1)S(1)}, bf16[512,512]{1,0:T(8,128)(2,1)}, u32[]{:S(2)}) copy-start(bf16[512,512]{1,0:T(8,128)(2,1)} %param.23) | copy-start | bytes 1572868
  705.8 39.3 %copy-start.4 = (f32[2,8,16,8,512]{4,3,2,1,0:T(8,128)S(1)}, f32[2,8,16,8,512]{4,3,2,1,0:T(8,128)}, u32[]{:S(2)}) copy-start(f32[2,8,16,8,512]{4,3,2,1,0:T(8,128)} %get-tuple-element.130) | copy-start | bytes 12582916
  705.8 39.3 %copy-start.14 = (bf16[2048,512]{1,0:T(8,128)(2,1)S(1)}, bf16[2048,512]{1,0:T(8,128)(2,1)}, u32[]{:S(2)}) copy-start(bf16[2048,512]{1,0:T(8,128)(2,1)} %param.31) | copy-start | bytes 6291460
  (2 other events, 3.3 us)
Sparse Core Ops, SparseCore 0:
  18.5 358.3 all-gather.2
  378.6 304.1 all-gather.4
where the time goes:
time: 770 us; the launch traced here: 758 us
  waiting for transfers between devices  379 us (49%)
  matrix products  174 us (23%)
  local copies, waits for them, and re-layouts  125 us (16%)
  other arithmetic  37.4 us (5%)
  starting transfers between devices  25.7 us (3%)
  between operations  14.1 us (2%)
    all_gather x1, waiting for transfers between devices, body(): lax.all_gather(value_part, ('region', 'tile'), axis=0, tiled=True)  294 us
    dot_general x4, matrix products, attend_block(): jnp.einsum('hqk,khd->qhd', weights_bf, value_rows, preferred_element_type...  62.6 us
    ppermute x2, waiting for transfers between devices, with_halo(): lax.ppermute(lax.slice_in_dim(block, block.shape[dim] - width, None, axis...  58.8 us
    dot_general x1, matrix products, body(): jnp.dot(normed_mixed, mlp_in, preferred_element_type=jnp.float32)  39.3 us
    sub x4, matrix products, attend_block(): weights = jnp.exp(scores - row_max)  37.7 us
    ppermute x2, starting transfers between devices, with_halo(): lax.ppermute(lax.slice_in_dim(block, 0, width, axis=dim), axis, backward)  23.8 us
    all_gather x1, waiting for transfers between devices, body(): lax.all_gather(key_part, ('region', 'tile'), axis=0, tiled=True)  20.5 us
    slice x4, local copies, waits for them, and re-layouts, attend_block(): value_rows = window[..., model_width:].reshape(-1, HEADS, HEAD_DIM)  20.3 us
  transfers between devices with their start and end apart: 6, of which 4 were waited for; matrix products, arithmetic and copies ran while one was open for 34% of the time, Pallas kernels for 0%

commit v1 on v0

v1 whole, which is shorter than its diff:
```python
import functools
import math

import jax
import jax.numpy as jnp
import numpy as np
from jax import lax
from jax.experimental import pallas as pl
from jax.experimental.pallas import tpu as pltpu
from jax.sharding import PartitionSpec as P

F32, BF16 = jnp.float32, jnp.bfloat16
MESH = pl.DeviceIdType.MESH
HEADS = 8
EPS = 1e-6
BIG = 131072.0
LOG2E = math.log2(math.e)
TAIL = (
    -1.0002404059668364,
    -1.1475987944049173,
    -0.46737700467532134,
    -0.04592394901048988,
    0.005166375711832039,
    -0.00025544077122896525,
)
NT = (((1,), (1,)), ((), ()))


def mm(a, b):
    return jnp.dot(a, b, preferred_element_type=F32)


def gelu(x):
    z = jnp.abs(x)
    p = TAIL[5] * z + TAIL[4]
    for c in TAIL[3::-1]:
        p = p * z + c
    return jnp.maximum(x, 0.0) - z * jnp.exp2(p)


def block_ones():
    i = np.arange(256) // 64
    return jnp.asarray((i[:, None] == i[None, :]).astype(np.float32) / 64.0, BF16)


def key_tables():
    t = np.zeros((4, 8, 32, 128), np.float32)
    q = np.arange(16)
    for chunk in range(4):
        for row in range(8):
            away = np.abs(q - (8 * (chunk - 1) + row))
            t[chunk, row, :, 0:16] = np.where(away <= 7, 0.0, -BIG)[None, :]
        for col in range(32):
            t[chunk, :, col, 16:32] = np.where(np.abs(q - (col - 8)) <= 7, 0.0, -BIG)[None, :]
    return jnp.asarray(t.reshape(4, 256, 128), BF16)


def query_table():
    t = np.zeros((16, 16, 128), np.float32)
    for i in range(16):
        t[i, :, i] = 1.0
        t[:, i, 16 + i] = 1.0
    return jnp.asarray(t.reshape(256, 128), BF16)


def head_norm(p, ones):
    sq = (p * p).astype(BF16)
    ms = jnp.concatenate([mm(sq[:, :256], ones), mm(sq[:, 256:], ones)], axis=1)
    return (p * lax.rsqrt(ms + EPS)).astype(BF16)


def normalize(x):
    return x * lax.rsqrt(jnp.mean(x * x, axis=-1, keepdims=True) + EPS)


def queries_of(q_s, qt_ref, j, p):
    q = q_s[:, pl.ds(pl.multiple_of(16 * j, 16), 16), 128 * p : 128 * p + 128].reshape(256, 128)
    low = lax.broadcasted_iota(jnp.int32, (256, 128), 1) < 64
    zero = jnp.zeros_like(q)
    qt = qt_ref[...]
    return [
        jnp.concatenate([jnp.where(low, q, zero), qt], axis=1),
        jnp.concatenate([jnp.where(low, zero, q), qt], axis=1),
    ]


def chunk_of(ref, row, j, p, extra):
    cols = pl.ds(pl.multiple_of(16 * j, 16), 32)
    x = ref[row : row + 8, cols, 128 * p : 128 * p + 128].reshape(256, 128)
    return jnp.concatenate([x, extra], axis=1)


def soft(s, c):
    top = jnp.max(s, axis=-1, keepdims=True)
    return jnp.exp2((s - top) * c).astype(BF16), top * c


def merge(first, second):
    low = lax.broadcasted_iota(jnp.int32, first.shape, 1) < 64
    return jnp.where(low, first, second)


def attend_own(j, p, q_s, k_s, v_s, qt_ref, kt_ref, c_ref, o_s, l_s, m_s):
    qa, qb = queries_of(q_s, qt_ref, j, p)
    ones = jnp.ones((256, 128), BF16)
    keys = jnp.concatenate([chunk_of(k_s, 8 * i, j, p, kt_ref[1 + i]) for i in range(2)], axis=0)
    vals = jnp.concatenate([chunk_of(v_s, 8 * i, j, p, ones) for i in range(2)], axis=0)
    s = lax.dot_general(jnp.concatenate([qa, qb], axis=0), keys, NT, preferred_element_type=F32)
    wa, ma = soft(s[:256], c_ref[2 * p])
    wb, mb = soft(s[256:], c_ref[2 * p + 1])
    o = mm(jnp.concatenate([wa, wb], axis=0), vals)
    o_s[j, p] = merge(o[:256, :128], o[256:, :128])
    l_s[j, p] = merge(o[:256, 128:], o[256:, 128:])
    m_s[j, p] = merge(jnp.broadcast_to(ma, (256, 128)), jnp.broadcast_to(mb, (256, 128)))


def attend_all(j, p, q_s, ku_s, kd_s, vu_s, vd_s, qt_ref, kt_ref, c_ref, o_s, l_s, m_s):
    qa, qb = queries_of(q_s, qt_ref, j, p)
    ones = jnp.ones((256, 128), BF16)
    done = []
    for k_s, v_s, table, part in ((ku_s, vu_s, 0, slice(0, 128)), (kd_s, vd_s, 3, slice(128, 256))):
        keys = chunk_of(k_s, 0, j, p, kt_ref[table])
        vals = chunk_of(v_s, 0, j, p, ones)
        q = jnp.concatenate([qa[part], qb[part]], axis=0)
        s = lax.dot_general(q, keys, NT, preferred_element_type=F32)
        wa, ma = soft(s[:128], c_ref[2 * p])
        wb, mb = soft(s[128:], c_ref[2 * p + 1])
        o = mm(jnp.concatenate([wa, wb], axis=0), vals)
        o2 = merge(o[:128, :128], o[128:, :128])
        l2 = merge(o[:128, 128:], o[128:, 128:])
        m2 = merge(jnp.broadcast_to(ma, (128, 128)), jnp.broadcast_to(mb, (128, 128)))
        o1, l1, m1 = o_s[j, p, part], l_s[j, p, part], m_s[j, p, part]
        top = jnp.maximum(m1, m2)
        a1, a2 = jnp.exp2(m1 - top), jnp.exp2(m2 - top)
        done.append(((o1 * a1 + o2 * a2) / (l1 * a1 + l2 * a2)).astype(BF16))
    return jnp.concatenate(done, axis=0)


def project(n, wk_ref, wv_ref, ones):
    return head_norm(mm(n, wk_ref[...]), ones), mm(n, wv_ref[...]).astype(BF16)


def project_own(i, buf, wq_ref, wk_ref, wv_ref, ones, q_s, k_s, v_s):
    wide = buf[i]
    q_s[i] = head_norm(mm(wide[16:144], wq_ref[...]), ones)
    n = wide.astype(F32)[8:152].astype(BF16)
    k_s[i], v_s[i] = project(n, wk_ref, wv_ref, ones)


def project_halo(k, buf, wk_ref, wv_ref, ones, k_s, v_s):
    n = buf[:, pl.ds(pl.multiple_of(32 * k, 32), 48), :].astype(F32)[:, 8:40].astype(BF16)
    keys, vals = project(n.reshape(256, 512), wk_ref, wv_ref, ones)
    cols = pl.ds(pl.multiple_of(32 * k, 32), 32)
    k_s[:, cols, :] = keys.reshape(8, 32, 512)
    v_s[:, cols, :] = vals.reshape(8, 32, 512)


def stream_of(tok, mask, emb):
    m = mask.astype(F32)
    return tok.astype(F32) + jnp.concatenate([m] * 4, axis=1) * emb


def finish(j, fine, tok_ref, mask_ref, emb_ref, fb_s, wo_ref, w1_ref, w2_ref, out_ref):
    at = pl.ds(pl.multiple_of(16 * j, 16), 16)
    stream = stream_of(tok_ref[:, at, :].reshape(256, 512), mask_ref[:, at, :].reshape(256, 128), emb_ref[...])
    fb = fb_s[:, pl.ds(2 * j, 2)].reshape(2, 1, 16, 512)
    fb = jnp.broadcast_to(fb, (2, 8, 16, 512)).reshape(256, 512)
    mixed = stream + mm(fine, wo_ref[...]) + fb
    nm = normalize(mixed).astype(BF16)
    acc = mixed
    for f in range(4):
        part = slice(512 * f, 512 * f + 512)
        h = gelu(mm(nm, w1_ref[:, part])).astype(BF16)
        acc = acc + mm(h, w2_ref[part, :])
    out_ref[:, at, :] = acc.astype(BF16).reshape(16, 16, 512)


LEFT, OWN, RIGHT = pl.ds(0, 16), pl.ds(16, 128), pl.ds(144, 16)
FIRST, LAST = pl.ds(16, 16), pl.ds(128, 16)
N_COPIES = 42


def layer(
    tok_ref, mask_ref, emb_ref, wq_ref, wk_ref, wv_ref, wo_ref, cwq_ref, cwk_ref, cwv_ref, cwo_ref,
    w1_ref, w2_ref, ones_ref, qt_ref, kt_ref, c_ref, cc_ref, out_ref,
    buf, up_buf, dn_buf, q_s, k_s, v_s, ku_s, vu_s, kd_s, vd_s, o_s, l_s, m_s,
    psum, cin_s, cq_s, x_s, ck_s, cv_s, qz_s, po_s, ps_s, rz_s, rs_s, fb_s, send_sem, recv_sem,
):
    t, r = lax.axis_index("tile"), lax.axis_index("region")
    prev, following = (t + 31) % 32, (t + 1) % 32
    left, right = (r + 3) % 4, (r + 1) % 4
    g, z_lo = t // 2, t % 2
    z_hi, core = r // 2, r % 2
    z = 2 * z_hi + z_lo
    ones = ones_ref[...]

    def plane(step):
        return {"tile": 2 * ((g + step) % 16) + z_lo, "region": r}

    def column(step):
        other = (z + step) % 4
        return {"tile": 2 * g + other % 2, "region": 2 * (other // 2) + core}

    def copy(src, dst, index, where):
        return pltpu.make_async_remote_copy(
            src_ref=src, dst_ref=dst, send_sem=send_sem.at[index], recv_sem=recv_sem.at[index],
            device_id=where, device_id_type=MESH,
        )

    to_left, to_right = {"tile": t, "region": left}, {"tile": t, "region": right}
    barrier = pltpu.get_barrier_semaphore()
    for where in [to_left, to_right] + [{"tile": a, "region": b} for a in (prev, following) for b in (left, r, right)]:
        pl.semaphore_signal(barrier, inc=1, device_id=where, device_id_type=MESH)

    @pl.loop(1, 16)
    def _(step):
        pl.semaphore_signal(barrier, inc=1, device_id=plane(step), device_id_type=MESH)

    for step in (1, 2, 3):
        pl.semaphore_signal(barrier, inc=1, device_id=column(step), device_id_type=MESH)

    psum[...] = jnp.zeros_like(psum)

    @pl.loop(0, 16)
    def _(i):
        n = normalize(stream_of(tok_ref[i], mask_ref[i], emb_ref[...])).astype(BF16)
        buf[i, OWN, :] = n
        psum[i // 8] += n.astype(F32)

    up_buf[0] = jnp.zeros((176, 512), BF16)
    dn_buf[7] = jnp.zeros((176, 512), BF16)

    pl.semaphore_wait(barrier, 26)

    top, bottom = pl.ds(0, 7), pl.ds(9, 7)
    up_rows, dn_rows = pl.ds(1, 7), pl.ds(0, 7)
    sides = [
        copy(buf.at[:, FIRST, :], buf.at[:, RIGHT, :], 0, to_left),
        copy(buf.at[:, LAST, :], buf.at[:, LEFT, :], 1, to_right),
    ]
    corners = [
        copy(buf.at[top, LAST, :], dn_buf.at[dn_rows, LEFT, :], 2, {"tile": prev, "region": right}),
        copy(buf.at[bottom, LAST, :], up_buf.at[up_rows, LEFT, :], 3, {"tile": following, "region": right}),
        copy(buf.at[top, FIRST, :], dn_buf.at[dn_rows, RIGHT, :], 4, {"tile": prev, "region": left}),
        copy(buf.at[bottom, FIRST, :], up_buf.at[up_rows, RIGHT, :], 5, {"tile": following, "region": left}),
    ]

    def row_piece(k):
        cols = pl.ds(pl.multiple_of(16 + 32 * k, 16), 32)
        return (
            copy(buf.at[top, cols, :], dn_buf.at[dn_rows, cols, :], 6 + k, {"tile": prev, "region": r}),
            copy(buf.at[bottom, cols, :], up_buf.at[up_rows, cols, :], 10 + k, {"tile": following, "region": r}),
        )

    for c in sides + corners:
        c.start()

    @pl.loop(0, 4)
    def _(k):
        for c in row_piece(k):
            c.start()

    cin = normalize(jnp.sum(psum[...].reshape(32, 8, 512), axis=1) * (1.0 / 64.0)).astype(BF16)
    cin_s[...] = cin
    x_s[core, g] = cin

    def gather(step):
        return copy(cin_s, x_s.at[core, g], 13 + step, plane(step))

    @pl.loop(1, 16)
    def _(step):
        gather(step).start()

    cq = head_norm(mm(cin, cwq_ref[...]), ones)
    cq_s[...] = cq
    qz_s[z] = cq
    asks = [copy(cq_s, qz_s.at[z], 28 + step, column(step)) for step in (1, 2, 3)]
    for c in asks:
        c.start()

    @pl.loop(0, 16)
    def _(i):
        q_s[i] = head_norm(mm(buf[i, OWN, :], wq_ref[...]), ones)

    for c in sides:
        c.wait_recv()

    @pl.loop(0, 16)
    def _(i):
        n = buf[i].astype(F32)[8:152].astype(BF16)
        k_s[i], v_s[i] = project(n, wk_ref, wv_ref, ones)

    @pl.loop(1, 16)
    def _(step):
        gather(step).wait_recv()

    sibling = copy(x_s.at[core], x_s.at[core], 32, {"tile": t, "region": 2 * z_hi + 1 - core})
    sibling.start()

    @pl.loop(0, 4)
    def _(j):
        for p in range(4):
            attend_own(j, p, q_s, k_s, v_s, qt_ref, kt_ref, c_ref, o_s, l_s, m_s)

    sibling.wait_recv()
    for c in asks:
        c.wait_recv()
    coarse_part(x_s, qz_s, cwk_ref, cwv_ref, cc_ref, ones, ck_s, cv_s, po_s, ps_s)
    replies = []
    for step in (1, 2, 3):
        rows = pl.ds(pl.multiple_of(32 * ((z + step) % 4), 32), 32)
        replies.append(copy(po_s.at[rows, :], rz_s.at[z], 32 + step, column(step)))
        replies.append(copy(ps_s.at[:, rows, :], rs_s.at[z], 35 + step, column(step)))
    for c in replies:
        c.start()
    mine = pl.ds(pl.multiple_of(32 * z, 32), 32)
    rz_s[z] = po_s[mine, :]
    rs_s[z] = ps_s[:, mine, :]

    @pl.loop(4, 8)
    def _(j):
        for p in range(4):
            attend_own(j, p, q_s, k_s, v_s, qt_ref, kt_ref, c_ref, o_s, l_s, m_s)

    for c in replies:
        c.wait_recv()
    feedback = mm(coarse_join(rz_s, rs_s), cwo_ref[...])
    fb_s[...] = jnp.broadcast_to(feedback.reshape(32, 1, 512), (32, 8, 512)).reshape(2, 16, 8, 512)

    def halo(k):
        project_halo(k, up_buf, wk_ref, wv_ref, ones, ku_s, vu_s)
        project_halo(k, dn_buf, wk_ref, wv_ref, ones, kd_s, vd_s)

    for c in corners[:2]:
        c.wait_recv()
    for c in row_piece(0):
        c.wait_recv()
    halo(0)

    @pl.loop(0, 8)
    def _(j):
        @pl.when(j % 2 == 1)
        def _():
            k = (j + 1) // 2

            @pl.when(j < 7)
            def _():
                for c in row_piece(k):
                    c.wait_recv()

            @pl.when(j == 7)
            def _():
                for c in corners[2:]:
                    c.wait_recv()

            halo(k)

        fine = jnp.concatenate(
            [
                attend_all(j, p, q_s, ku_s, kd_s, vu_s, vd_s, qt_ref, kt_ref, c_ref, o_s, l_s, m_s)
                for p in range(4)
            ],
            axis=1,
        )
        finish(j, fine, tok_ref, mask_ref, emb_ref, fb_s, wo_ref, w1_ref, w2_ref, out_ref)

    for c in sides + corners + asks + [sibling] + replies:
        c.wait_send()

    @pl.loop(0, 4)
    def _(k):
        for c in row_piece(k):
            c.wait_send()

    @pl.loop(1, 16)
    def _(step):
        gather(step).wait_send()


def coarse_part(x_s, qz_s, wk_ref, wv_ref, cc_ref, ones, ck_s, cv_s, po_s, ps_s):
    @pl.loop(0, 4)
    def _(i):
        x = x_s[i // 2, pl.ds(8 * (i % 2), 8)].reshape(256, 512)
        rows = pl.ds(pl.multiple_of(256 * i, 256), 256)
        k, v = project(x, wk_ref, wv_ref, ones)
        ck_s[rows, :] = k
        cv_s[rows, :] = v

    q = qz_s[...].reshape(128, 512)
    lane = lax.broadcasted_iota(jnp.int32, (128, 128), 1)
    head = lax.broadcasted_iota(jnp.int32, (128, 256), 1) // 64
    tops = jnp.zeros((128, 128), F32)
    sums = jnp.zeros((128, 128), F32)
    for half in range(2):
        lanes = slice(256 * half, 256 * half + 256)
        qh = q[:, lanes]
        rows = jnp.concatenate([jnp.where(head == h, qh, jnp.zeros_like(qh)) for h in range(4)], axis=0)
        s = lax.dot_general(rows, ck_s[:, lanes], NT, preferred_element_type=F32)
        weights = []
        for h in range(4):
            c = cc_ref[4 * half + h]
            part = s[128 * h : 128 * h + 128]
            top = jnp.max(part, axis=-1, keepdims=True)
            w = jnp.exp2((part - top) * c)
            tops = jnp.where(lane == 4 * half + h, top * c, tops)
            sums = jnp.where(lane == 4 * half + h, jnp.sum(w, axis=-1, keepdims=True), sums)
            weights.append(w.astype(BF16))
        o = mm(jnp.concatenate(weights, axis=0), cv_s[:, lanes])
        picked = o[:128]
        for h in range(1, 4):
            picked = jnp.where(head == h, o[128 * h : 128 * h + 128], picked)
        po_s[:, lanes] = picked
    ps_s[0] = tops
    ps_s[1] = sums


def coarse_join(rz_s, rs_s):
    top = jnp.maximum(jnp.maximum(rs_s[0, 0], rs_s[1, 0]), jnp.maximum(rs_s[2, 0], rs_s[3, 0]))
    scale = [jnp.exp2(rs_s[i, 0] - top) for i in range(4)]
    total = sum(scale[i] * rs_s[i, 1] for i in range(4))
    low = lax.broadcasted_iota(jnp.int32, (32, 128), 1) < 64
    joined = jnp.zeros((32, 512), F32)
    for i in range(4):
        a = scale[i] / total
        wide = [
            jnp.where(low, jnp.broadcast_to(a[:, 2 * p : 2 * p + 1], (32, 128)), jnp.broadcast_to(a[:, 2 * p + 1 : 2 * p + 2], (32, 128)))
            for p in range(4)
        ]
        joined = joined + jnp.concatenate(wide, axis=1) * rz_s[i]
    return joined.astype(BF16)


def body(
    tokens, pore_mask, solid_embed, fine_query, fine_key, fine_value, fine_out, fine_scale,
    coarse_query, coarse_key, coarse_value, coarse_out, coarse_scale, mlp_in, mlp_out,
):
    mask = jnp.broadcast_to(pore_mask.astype(BF16)[..., None], (16, 128, 128))
    factor = LOG2E / math.sqrt(64)
    vm = pl.BlockSpec(memory_space=pltpu.VMEM)
    sm = pl.BlockSpec(memory_space=pltpu.SMEM)
    V = pltpu.VMEM
    return pl.pallas_call(
        layer,
        out_shape=jax.ShapeDtypeStruct((16, 128, 512), BF16),
        in_specs=[vm] * 16 + [sm] * 2,
        out_specs=vm,
        scratch_shapes=[
            V((16, 160, 512), BF16),
            V((8, 176, 512), BF16),
            V((8, 176, 512), BF16),
            V((16, 128, 512), BF16),
            V((16, 144, 512), BF16),
            V((16, 144, 512), BF16),
            V((8, 160, 512), BF16),
            V((8, 160, 512), BF16),
            V((8, 160, 512), BF16),
            V((8, 160, 512), BF16),
            V((8, 4, 256, 128), F32),
            V((8, 4, 256, 128), F32),
            V((8, 4, 256, 128), F32),
            V((2, 128, 512), F32),
            V((32, 512), BF16),
            V((32, 512), BF16),
            V((2, 16, 32, 512), BF16),
            V((1024, 512), BF16),
            V((1024, 512), BF16),
            V((4, 32, 512), BF16),
            V((128, 512), F32),
            V((2, 128, 128), F32),
            V((4, 32, 512), F32),
            V((4, 2, 32, 128), F32),
            V((2, 16, 8, 512), F32),
            pltpu.SemaphoreType.DMA((N_COPIES,)),
            pltpu.SemaphoreType.DMA((N_COPIES,)),
        ],
        compiler_params=pltpu.CompilerParams(
            collective_id=0, has_side_effects=True, vmem_limit_bytes=62 * 2**20
        ),
    )(
        tokens, mask, solid_embed.reshape(1, 512), fine_query, fine_key, fine_value, fine_out,
        coarse_query, coarse_key, coarse_value, coarse_out, mlp_in, mlp_out,
        block_ones(), query_table(), key_tables(), fine_scale * factor, coarse_scale * factor,
    )


def solution(mesh):
    placed = (P("tile", "region", None), P("tile", "region")) + (P(),) * 13
    return jax.shard_map(
        body, mesh=mesh, in_specs=placed, out_specs=P("tile", "region", None), check_vma=False
    )
```

time: 770 us -> 123 us (0.16); the launches traced: 758 us -> 123 us
  waiting for transfers between devices: 379 us -> 0 us
  matrix products: 174 us -> 0 us
  local copies, waits for them, and re-layouts: 125 us -> 4.23 us
  Pallas kernels: 0 us -> 117 us
  other arithmetic: 37.4 us -> 1.92 us
  starting transfers between devices: 25.7 us -> 0 us
  between operations: 14.1 us -> 0.01 us
    all_gather x2 -> x0, waiting for transfers between devices: 314 us -> none  [the longest x1 294 us: body(): lax.all_gather(value_part, ('region', 'tile'), axis=0, tiled=True)]
    dot_general x16 -> x0, matrix products: 136 us -> none  [the longest x4 62.6 us: attend_block(): jnp.einsum('hqk,khd->qhd', weights_bf, value_rows, preferred_element_type...]
    pallas_call x0 -> x1, Pallas kernels: none -> 117 us  [body(): pl.pallas_call(layer, out_shape=jax.ShapeDtypeStruct((16, 128, 512), BF16...]
    ppermute x4 -> x0, waiting for transfers between devices: 64.4 us -> none  [the longest x2 58.8 us: with_halo(): lax.ppermute(lax.slice_in_dim(block, block.shape[dim] - width, None, axis...]
    reshape x13 -> x0, local copies, waits for them, and re-layouts: 48.5 us -> none  [the longest x4 18.1 us: attend_block(): value_rows = window[..., model_width:].reshape(-1, HEADS, HEAD_DIM)]
    sub x4 -> x0, matrix products: 37.7 us -> none  [attend_block(): weights = jnp.exp(scores - row_max)]
    ppermute x4 -> x0, starting transfers between devices: 25.6 us -> none  [the longest x2 23.8 us: with_halo(): lax.ppermute(lax.slice_in_dim(block, 0, width, axis=dim), axis, backward)]
    slice x5 -> x0, local copies, waits for them, and re-layouts: 22.1 us -> none  [the longest x4 20.3 us: attend_block(): value_rows = window[..., model_width:].reshape(-1, HEADS, HEAD_DIM)]
  transfers between devices with their start and end apart: 6 -> 0, of which waited for: 4 -> 0; matrix products, arithmetic and copies ran while one was open for 34% -> 0% of each run, Pallas kernels for 0% -> 0%
where the time goes in v1:
time: 123 us
  Pallas kernels  117 us (95%)
  local copies, waits for them, and re-layouts  4.23 us (3%)
  other arithmetic  1.92 us (2%)
    pallas_call x1, Pallas kernels, body(): pl.pallas_call(layer, out_shape=jax.ShapeDtypeStruct((16, 128, 512), BF16...  117 us
    unnamed x1, local copies, waits for them, and re-layouts  3.1 us

profile of v1, /device:TPU:0, one launch (start us, length us, event | category | flops | bytes accessed | tf_op | source)
XLA Modules:
  0.0 122.7 jit_solution(11874027715726764234)
XLA Ops:
  0.0 1.2 broadcast_multiply_fusion
  1.2 0.7 convert_element_type.3
  1.9 1.1 broadcast_in_dim.2.mask_ref
  3.1 116.6 %shard_map.172 = bf16[16,128,512]{2,1,0:T(8,128)(2,1)} custom-call(bf16[16,128,512]{2,1,0:T(8,128)(2,1)} %tok_ref.1, bf16[16,128,128]{2,1,0:T(8,128)(2,1)} %broadcast_in_dim.2.mask_ref, f32[1,512]{1,0:T(1,128)} %bitcast.1, bf16[512,512]{1,0:T(8,128)(2,1)} %wq_ref.1, bf16[512,512]{1,0:T(8,128)(2,1)} %wk_ref.1, bf16[512,512]{1,0:T(8,128)(2,1)} %wv_ref.1, ...), custom_call_target="tpu_custom_call" | custom-call | tf_op jit(solution)/shard_map/pallas_call | solution.py:442
  119.6 3.1 %copy.20 = bf16[16,128,512]{2,1,0:T(8,128)(2,1)} copy(bf16[16,128,512]{2,1,0:T(8,128)(2,1)} %shard_map.172) | data formatting | bytes 4194304

commit v2 on v1

v2 whole, which is shorter than its diff:
```python
import functools
import math

import jax
import jax.numpy as jnp
import numpy as np
from jax import lax
from jax.experimental import pallas as pl
from jax.experimental.pallas import tpu as pltpu
from jax.sharding import PartitionSpec as P

F32, BF16 = jnp.float32, jnp.bfloat16
MESH = pl.DeviceIdType.MESH
HEADS = 8
EPS = 1e-6
BIG = 131072.0
FACTOR = math.log2(math.e) / 8.0
TAIL = (
    -1.0002404059668364,
    -1.1475987944049173,
    -0.46737700467532134,
    -0.04592394901048988,
    0.005166375711832039,
    -0.00025544077122896525,
)
NT = (((1,), (1,)), ((), ()))


def mm(a, b):
    return jnp.dot(a, b, preferred_element_type=F32)


def gelu(x):
    z = jnp.abs(x)
    p = TAIL[5] * z + TAIL[4]
    for c in TAIL[3::-1]:
        p = p * z + c
    return jnp.maximum(x, 0.0) - z * jnp.exp2(p)


def block_ones():
    i = np.arange(256) // 64
    return jnp.asarray((i[:, None] == i[None, :]).astype(np.float32) / 64.0, BF16)


def key_tables():
    t = np.zeros((4, 8, 32, 128), np.float32)
    q = np.arange(16)
    for chunk in range(4):
        for row in range(8):
            away = np.abs(q - (8 * (chunk - 1) + row))
            t[chunk, row, :, 0:16] = np.where(away <= 7, 0.0, -BIG)[None, :]
        for col in range(32):
            t[chunk, :, col, 16:32] = np.where(np.abs(q - (col - 8)) <= 7, 0.0, -BIG)[None, :]
    return jnp.asarray(t.reshape(4, 256, 128), BF16)


def query_table():
    t = np.zeros((16, 16, 128), np.float32)
    for i in range(16):
        t[i, :, i] = 1.0
        t[:, i, 16 + i] = 1.0
    return jnp.asarray(t.reshape(256, 128), BF16)


def head_norm(p, ones):
    sq = (p * p).astype(BF16)
    ms = jnp.concatenate([mm(sq[:, :256], ones), mm(sq[:, 256:], ones)], axis=1)
    return (p * lax.rsqrt(ms + EPS)).astype(BF16)


def normalize(x):
    return x * lax.rsqrt(jnp.mean(x * x, axis=-1, keepdims=True) + EPS)


def queries_of(q_s, qt_ref, j, p):
    q = q_s[:, pl.ds(pl.multiple_of(16 * j, 16), 16), 128 * p : 128 * p + 128].reshape(256, 128)
    low = lax.broadcasted_iota(jnp.int32, (256, 128), 1) < 64
    zero = jnp.zeros_like(q)
    qt = qt_ref[...]
    return [
        jnp.concatenate([jnp.where(low, q, zero), qt], axis=1),
        jnp.concatenate([jnp.where(low, zero, q), qt], axis=1),
    ]


def chunk_of(ref, row, j, p, extra):
    cols = pl.ds(pl.multiple_of(16 * j, 16), 32)
    x = ref[row : row + 8, cols, 128 * p : 128 * p + 128].reshape(256, 128)
    return jnp.concatenate([x, extra], axis=1)


def soft(s, c):
    top = jnp.max(s, axis=-1, keepdims=True)
    return jnp.exp2((s - top) * c).astype(BF16), top * c


def merge(first, second):
    low = lax.broadcasted_iota(jnp.int32, first.shape, 1) < 64
    return jnp.where(low, first, second)


def attend_own(j, p, q_s, k_s, v_s, qt_ref, kt_ref, c_ref, o_s, l_s, m_s):
    qa, qb = queries_of(q_s, qt_ref, j, p)
    ones = jnp.ones((256, 128), BF16)
    keys = jnp.concatenate([chunk_of(k_s, 8 * i, j, p, kt_ref[1 + i]) for i in range(2)], axis=0)
    vals = jnp.concatenate([chunk_of(v_s, 8 * i, j, p, ones) for i in range(2)], axis=0)
    s = lax.dot_general(jnp.concatenate([qa, qb], axis=0), keys, NT, preferred_element_type=F32)
    wa, ma = soft(s[:256], c_ref[2 * p])
    wb, mb = soft(s[256:], c_ref[2 * p + 1])
    o = mm(jnp.concatenate([wa, wb], axis=0), vals)
    o_s[j, p] = merge(o[:256, :128], o[256:, :128])
    l_s[j, p] = merge(o[:256, 128:], o[256:, 128:])
    m_s[j, p] = merge(jnp.broadcast_to(ma, (256, 128)), jnp.broadcast_to(mb, (256, 128)))


def attend_all(j, p, q_s, ku_s, kd_s, vu_s, vd_s, qt_ref, kt_ref, c_ref, o_s, l_s, m_s):
    qa, qb = queries_of(q_s, qt_ref, j, p)
    ones = jnp.ones((256, 128), BF16)
    done = []
    for k_s, v_s, table, part in ((ku_s, vu_s, 0, slice(0, 128)), (kd_s, vd_s, 3, slice(128, 256))):
        keys = chunk_of(k_s, 0, j, p, kt_ref[table])
        vals = chunk_of(v_s, 0, j, p, ones)
        q = jnp.concatenate([qa[part], qb[part]], axis=0)
        s = lax.dot_general(q, keys, NT, preferred_element_type=F32)
        wa, ma = soft(s[:128], c_ref[2 * p])
        wb, mb = soft(s[128:], c_ref[2 * p + 1])
        o = mm(jnp.concatenate([wa, wb], axis=0), vals)
        o2 = merge(o[:128, :128], o[128:, :128])
        l2 = merge(o[:128, 128:], o[128:, 128:])
        m2 = merge(jnp.broadcast_to(ma, (128, 128)), jnp.broadcast_to(mb, (128, 128)))
        o1, l1, m1 = o_s[j, p, part], l_s[j, p, part], m_s[j, p, part]
        top = jnp.maximum(m1, m2)
        a1, a2 = jnp.exp2(m1 - top), jnp.exp2(m2 - top)
        done.append(((o1 * a1 + o2 * a2) / (l1 * a1 + l2 * a2)).astype(BF16))
    return jnp.concatenate(done, axis=0)


def project(n, wk, wv, ones):
    return head_norm(mm(n, wk), ones), mm(n, wv).astype(BF16)


def stream_of(tok, mask, emb):
    m = mask.astype(F32)
    return tok.astype(F32) + jnp.concatenate([m] * 4, axis=1) * emb


def finish(start, cols, fine_s, tok_s, mask_s, emb_ref, fb_s, wo, w1_s, w2_s, out_s):
    count = 16 * cols
    at = pl.ds(pl.multiple_of(start, 16), cols)
    stream = stream_of(tok_s[:, at, :].reshape(count, 512), mask_s[:, at, :].reshape(count, 128), emb_ref[...])
    fb = fb_s[:, pl.ds(start // 8, cols // 8)].reshape(2, 1, cols, 512)
    fb = jnp.broadcast_to(fb, (2, 8, cols, 512)).reshape(count, 512)
    mixed = stream + mm(fine_s[:, at, :].reshape(count, 512), wo) + fb
    nm = normalize(mixed).astype(BF16)
    acc = mixed
    for f in range(4):
        part = slice(512 * f, 512 * f + 512)
        h = gelu(mm(nm, w1_s[:, part])).astype(BF16)
        acc = acc + mm(h, w2_s[part, :])
    out_s[:, at, :] = acc.astype(BF16).reshape(16, cols, 512)


LEFT, RIGHT, REST = pl.ds(0, 16), pl.ds(144, 16), pl.ds(160, 16)
N_COPIES = 42
QUERY, KEY, VALUE, OUT, CQUERY, CKEY, CVALUE, COUT = range(8)


def layer(
    tok_ref, mask_ref, emb_ref, wq_ref, wk_ref, wv_ref, wo_ref, cwq_ref, cwk_ref, cwv_ref, cwo_ref,
    w1_ref, w2_ref, ones_ref, qt_ref, kt_ref, scale_ref, cscale_ref, out_ref,
    tok_s, mask_s, w_s, w1_s, w2_s, out_s, fine_s,
    buf, ls_s, rs_s, lr_s, rr_s, corner_s, up_buf, dn_buf, q_s, k_s, v_s, ku_s, vu_s, kd_s, vd_s, o_s, l_s, m_s,
    psum, cin_s, cq_s, x_s, ck_s, cv_s, qz_s, po_s, ps_s, rz_s, rst_s, fb_s, c_ref, cc_ref,
    send_sem, recv_sem, load_sem, store_sem,
):
    t, r = lax.axis_index("tile"), lax.axis_index("region")
    prev, following = (t + 31) % 32, (t + 1) % 32
    left, right = (r + 3) % 4, (r + 1) % 4
    g, z_lo = t // 2, t % 2
    z_hi, core = r // 2, r % 2
    z = 2 * z_hi + z_lo

    def plane(step):
        return {"tile": 2 * ((g + step) % 16) + z_lo, "region": r}

    def column(step):
        other = (z + step) % 4
        return {"tile": 2 * g + other % 2, "region": 2 * (other // 2) + core}

    def copy(src, dst, index, where):
        return pltpu.make_async_remote_copy(
            src_ref=src, dst_ref=dst, send_sem=send_sem.at[index], recv_sem=recv_sem.at[index],
            device_id=where, device_id_type=MESH,
        )

    load_tok = pltpu.make_async_copy(tok_ref, tok_s, load_sem.at[0])
    load_tok.start()
    names = (wq_ref, wk_ref, wv_ref, wo_ref, cwq_ref, cwk_ref, cwv_ref, cwo_ref)
    loads = [pltpu.make_async_copy(ref, w_s.at[i], load_sem.at[1 + i]) for i, ref in enumerate(names)]
    load_1 = pltpu.make_async_copy(w1_ref, w1_s, load_sem.at[9])
    load_2 = pltpu.make_async_copy(w2_ref, w2_s, load_sem.at[10])
    for i in (CQUERY, QUERY, KEY, VALUE, CKEY, CVALUE, OUT, COUT):
        loads[i].start()
    load_1.start()
    load_2.start()

    barrier = pltpu.get_barrier_semaphore()
    to_left, to_right = {"tile": t, "region": left}, {"tile": t, "region": right}
    for where in [to_left, to_right] + [{"tile": a, "region": b} for a in (prev, following) for b in (left, r, right)]:
        pl.semaphore_signal(barrier, inc=1, device_id=where, device_id_type=MESH)

    @pl.loop(1, 16)
    def _(step):
        pl.semaphore_signal(barrier, inc=1, device_id=plane(step), device_id_type=MESH)

    for step in (1, 2, 3):
        pl.semaphore_signal(barrier, inc=1, device_id=column(step), device_id_type=MESH)

    ones = ones_ref[...]
    for h in range(HEADS):
        c_ref[h] = scale_ref[h] * FACTOR
        cc_ref[h] = cscale_ref[h] * FACTOR
    psum[...] = jnp.zeros_like(psum)
    up_buf[0] = jnp.zeros((176, 512), BF16)
    dn_buf[7] = jnp.zeros((176, 512), BF16)
    up_buf[:, REST, :] = jnp.zeros((8, 16, 512), BF16)
    dn_buf[:, REST, :] = jnp.zeros((8, 16, 512), BF16)
    load_tok.wait()

    @pl.loop(0, 8)
    def _(i):
        pair = []
        for s in range(2):
            row = 2 * i + s
            m = jnp.broadcast_to(mask_ref[pl.ds(row, 1), :].astype(F32), (128, 128)).T.astype(BF16)
            mask_s[row] = m
            n = normalize(stream_of(tok_s[row], m, emb_ref[...]))
            nb = n.astype(BF16)
            buf[row] = nb
            psum[i // 4] += nb.astype(F32)
            pair.append(n)
        at = pl.ds(pl.multiple_of(16 * i, 16), 16)
        ls_s[at, :] = jnp.concatenate([n[:8] for n in pair], axis=0).astype(BF16)
        rs_s[at, :] = jnp.concatenate([n[120:] for n in pair], axis=0).astype(BF16)

    cin = normalize(jnp.sum(psum[...].reshape(32, 8, 512), axis=1) * (1.0 / 64.0)).astype(BF16)
    cin_s[...] = cin
    x_s[core, g] = cin

    pl.semaphore_wait(barrier, 26)

    sides = [copy(ls_s, rr_s, 0, to_left), copy(rs_s, lr_s, 1, to_right)]
    first, last = pl.ds(0, 64), pl.ds(64, 64)
    corners = [
        copy(rs_s.at[first, :], corner_s.at[0], 2, {"tile": prev, "region": right}),
        copy(rs_s.at[last, :], corner_s.at[1], 3, {"tile": following, "region": right}),
        copy(ls_s.at[first, :], corner_s.at[2], 4, {"tile": prev, "region": left}),
        copy(ls_s.at[last, :], corner_s.at[3], 5, {"tile": following, "region": left}),
    ]

    def row_piece(k):
        src = pl.ds(pl.multiple_of(32 * k, 16), 32)
        dst = pl.ds(pl.multiple_of(16 + 32 * k, 16), 32)
        return (
            copy(buf.at[pl.ds(0, 7), src, :], dn_buf.at[pl.ds(0, 7), dst, :], 6 + k, {"tile": prev, "region": r}),
            copy(buf.at[pl.ds(9, 7), src, :], up_buf.at[pl.ds(1, 7), dst, :], 10 + k, {"tile": following, "region": r}),
        )

    def gather(step):
        return copy(cin_s, x_s.at[core, g], 13 + step, plane(step))

    for c in sides:
        c.start()

    @pl.loop(1, 16)
    def _(step):
        gather(step).start()

    for c in corners[:2]:
        c.start()

    @pl.loop(0, 4)
    def _(k):
        for c in row_piece(k):
            c.start()

    for c in corners[2:]:
        c.start()

    loads[CQUERY].wait()
    cq = head_norm(mm(cin, w_s[CQUERY]), ones)
    cq_s[...] = cq
    qz_s[z] = cq
    asks = [copy(cq_s, qz_s.at[z], 28 + step, column(step)) for step in (1, 2, 3)]
    for c in asks:
        c.start()

    loads[QUERY].wait()

    @pl.loop(0, 4)
    def _(i):
        rows = pl.ds(4 * i, 4)
        q_s[rows] = head_norm(mm(buf[rows].reshape(512, 512), w_s[QUERY]), ones).reshape(4, 128, 512)

    loads[KEY].wait()
    loads[VALUE].wait()
    for c in sides:
        c.wait_recv()

    @pl.loop(0, 4)
    def _(i):
        rows = pl.ds(4 * i, 4)
        at = pl.ds(pl.multiple_of(32 * i, 32), 32)
        near = [ref[at, :].astype(F32).reshape(4, 8, 512) for ref in (lr_s, rr_s)]
        n = jnp.concatenate([near[0], buf[rows].astype(F32), near[1]], axis=1).astype(BF16)
        keys, vals = project(n.reshape(576, 512), w_s[KEY], w_s[VALUE], ones)
        k_s[rows] = keys.reshape(4, 144, 512)
        v_s[rows] = vals.reshape(4, 144, 512)

    @pl.loop(1, 16)
    def _(step):
        gather(step).wait_recv()

    sibling = copy(x_s.at[core], x_s.at[core], 32, {"tile": t, "region": 2 * z_hi + 1 - core})
    sibling.start()
    replies = []
    for step in (1, 2, 3):
        rows = pl.ds(pl.multiple_of(32 * ((z + step) % 4), 32), 32)
        replies.append(copy(po_s.at[rows, :], rz_s.at[z], 32 + step, column(step)))
        replies.append(copy(ps_s.at[:, rows, :], rst_s.at[z], 35 + step, column(step)))

    @pl.loop(0, 8)
    def _(j):
        @pl.when(j == 3)
        def _():
            sibling.wait_recv()
            for c in asks:
                c.wait_recv()
            loads[CKEY].wait()
            loads[CVALUE].wait()
            coarse_part(x_s, qz_s, w_s, cc_ref, ones, ck_s, cv_s, po_s, ps_s)
            for c in replies:
                c.start()
            mine = pl.ds(pl.multiple_of(32 * z, 32), 32)
            rz_s[z] = po_s[mine, :]
            rst_s[z] = ps_s[:, mine, :]

        for p in range(4):
            attend_own(j, p, q_s, k_s, v_s, qt_ref, kt_ref, c_ref, o_s, l_s, m_s)

    for c in replies:
        c.wait_recv()
    loads[COUT].wait()
    feedback = mm(coarse_join(rz_s, rst_s), w_s[COUT])
    fb_s[...] = jnp.broadcast_to(feedback.reshape(32, 1, 512), (32, 8, 512)).reshape(2, 16, 8, 512)
    loads[OUT].wait()
    load_1.wait()
    load_2.wait()

    def place(source, dst, where):
        x = source.astype(F32).reshape(8, 8, 512)
        zero = jnp.zeros_like(x)
        both = [zero, x] if where is LEFT else [x, zero]
        dst[:, where, :] = jnp.concatenate(both, axis=1).astype(BF16)

    def attend(j):
        fine = [
            attend_all(j, p, q_s, ku_s, kd_s, vu_s, vd_s, qt_ref, kt_ref, c_ref, o_s, l_s, m_s)
            for p in range(4)
        ]
        at = pl.ds(pl.multiple_of(16 * j, 16), 16)
        fine_s[:, at, :] = jnp.concatenate(fine, axis=1).reshape(16, 16, 512)

    def store(start, cols, index):
        at = pl.ds(pl.multiple_of(start, 16), cols)
        return pltpu.make_async_copy(out_s.at[:, at, :], out_ref.at[:, at, :], store_sem.at[index])

    def close(start, cols, index):
        finish(start, cols, fine_s, tok_s, mask_s, emb_ref, fb_s, w_s[OUT], w1_s, w2_s, out_s)
        store(start, cols, index).start()

    @pl.loop(0, 5)
    def _(i):
        @pl.when(i < 4)
        def _():
            for c in row_piece(i):
                c.wait_recv()

        @pl.when(i == 0)
        def _():
            for c in corners[:2]:
                c.wait_recv()
            place(corner_s[0], dn_buf, LEFT)
            place(corner_s[1], up_buf, LEFT)

        @pl.when(i == 4)
        def _():
            for c in corners[2:]:
                c.wait_recv()
            place(corner_s[2], dn_buf, RIGHT)
            place(corner_s[3], up_buf, RIGHT)

        src = pl.ds(pl.multiple_of(32 * i, 32), 48)
        cols = pl.ds(pl.multiple_of(32 * i, 32), 32)
        n = jnp.concatenate([b[:, src, :].astype(F32)[:, 8:40].astype(BF16) for b in (up_buf, dn_buf)], axis=0)
        keys, vals = project(n.reshape(512, 512), w_s[KEY], w_s[VALUE], ones)
        keys, vals = keys.reshape(16, 32, 512), vals.reshape(16, 32, 512)
        ku_s[:, cols, :], kd_s[:, cols, :] = keys[:8], keys[8:]
        vu_s[:, cols, :], vd_s[:, cols, :] = vals[:8], vals[8:]

        @pl.when(i > 0)
        def _():
            attend(2 * i - 1)

        @pl.when(i < 4)
        def _():
            attend(2 * i)

        @pl.when(i == 0)
        def _():
            close(0, 16, 0)

        @pl.when((i > 0) & (i < 4))
        def _():
            close(32 * i - 16, 32, i)

        @pl.when(i == 4)
        def _():
            close(112, 16, 4)

    store(0, 16, 0).wait()

    @pl.loop(1, 4)
    def _(i):
        store(32 * i - 16, 32, i).wait()

    store(112, 16, 4).wait()
    for c in sides + corners + asks + [sibling] + replies:
        c.wait_send()

    @pl.loop(0, 4)
    def _(k):
        for c in row_piece(k):
            c.wait_send()

    @pl.loop(1, 16)
    def _(step):
        gather(step).wait_send()


def coarse_part(x_s, qz_s, w_s, cc_ref, ones, ck_s, cv_s, po_s, ps_s):
    @pl.loop(0, 2)
    def _(i):
        x = x_s[i].reshape(512, 512)
        rows = pl.ds(pl.multiple_of(512 * i, 512), 512)
        k, v = project(x, w_s[CKEY], w_s[CVALUE], ones)
        ck_s[rows, :] = k
        cv_s[rows, :] = v

    q = qz_s[...].reshape(128, 512)
    lane = lax.broadcasted_iota(jnp.int32, (128, 128), 1)
    head = lax.broadcasted_iota(jnp.int32, (128, 256), 1) // 64
    tops = jnp.zeros((128, 128), F32)
    sums = jnp.zeros((128, 128), F32)
    for half in range(2):
        lanes = slice(256 * half, 256 * half + 256)
        qh = q[:, lanes]
        rows = jnp.concatenate([jnp.where(head == h, qh, jnp.zeros_like(qh)) for h in range(4)], axis=0)
        s = lax.dot_general(rows, ck_s[:, lanes], NT, preferred_element_type=F32)
        weights = []
        for h in range(4):
            c = cc_ref[4 * half + h]
            part = s[128 * h : 128 * h + 128]
            top = jnp.max(part, axis=-1, keepdims=True)
            w = jnp.exp2((part - top) * c)
            tops = jnp.where(lane == 4 * half + h, top * c, tops)
            sums = jnp.where(lane == 4 * half + h, jnp.sum(w, axis=-1, keepdims=True), sums)
            weights.append(w.astype(BF16))
        o = mm(jnp.concatenate(weights, axis=0), cv_s[:, lanes])
        picked = o[:128]
        for h in range(1, 4):
            picked = jnp.where(head == h, o[128 * h : 128 * h + 128], picked)
        po_s[:, lanes] = picked
    ps_s[0] = tops
    ps_s[1] = sums


def coarse_join(rz_s, rs_s):
    top = jnp.maximum(jnp.maximum(rs_s[0, 0], rs_s[1, 0]), jnp.maximum(rs_s[2, 0], rs_s[3, 0]))
    scale = [jnp.exp2(rs_s[i, 0] - top) for i in range(4)]
    total = sum(scale[i] * rs_s[i, 1] for i in range(4))
    low = lax.broadcasted_iota(jnp.int32, (32, 128), 1) < 64
    joined = jnp.zeros((32, 512), F32)
    for i in range(4):
        a = scale[i] / total
        wide = [
            jnp.where(low, jnp.broadcast_to(a[:, 2 * p : 2 * p + 1], (32, 128)), jnp.broadcast_to(a[:, 2 * p + 1 : 2 * p + 2], (32, 128)))
            for p in range(4)
        ]
        joined = joined + jnp.concatenate(wide, axis=1) * rz_s[i]
    return joined.astype(BF16)


def body(
    tokens, pore_mask, solid_embed, fine_query, fine_key, fine_value, fine_out, fine_scale,
    coarse_query, coarse_key, coarse_value, coarse_out, coarse_scale, mlp_in, mlp_out,
):
    vm = pl.BlockSpec(memory_space=pltpu.VMEM)
    sm = pl.BlockSpec(memory_space=pltpu.SMEM)
    hbm = pl.BlockSpec(memory_space=pl.ANY)

    def half(*shape):
        return pltpu.VMEM(shape, BF16)

    def full(*shape):
        return pltpu.VMEM(shape, F32)

    dma = pltpu.SemaphoreType.DMA
    return pl.pallas_call(
        layer,
        out_shape=jax.ShapeDtypeStruct((16, 128, 512), BF16),
        in_specs=[hbm, vm, vm] + [hbm] * 10 + [vm] * 3 + [sm] * 2,
        out_specs=hbm,
        scratch_shapes=[
            half(16, 128, 512),
            half(16, 128, 128),
            half(8, 512, 512),
            half(512, 2048),
            half(2048, 512),
            half(16, 128, 512),
            half(16, 128, 512),
            half(16, 128, 512),
            half(128, 512),
            half(128, 512),
            half(128, 512),
            half(128, 512),
            half(4, 64, 512),
            half(8, 176, 512),
            half(8, 176, 512),
            half(16, 128, 512),
            half(16, 144, 512),
            half(16, 144, 512),
            half(8, 160, 512),
            half(8, 160, 512),
            half(8, 160, 512),
            half(8, 160, 512),
            full(8, 4, 256, 128),
            full(8, 4, 256, 128),
            full(8, 4, 256, 128),
            full(2, 128, 512),
            half(32, 512),
            half(32, 512),
            half(2, 16, 32, 512),
            half(1024, 512),
            half(1024, 512),
            half(4, 32, 512),
            full(128, 512),
            full(2, 128, 128),
            full(4, 32, 512),
            full(4, 2, 32, 128),
            full(2, 16, 8, 512),
            pltpu.SMEM((8,), F32),
            pltpu.SMEM((8,), F32),
            dma((N_COPIES,)),
            dma((N_COPIES,)),
            dma((11,)),
            dma((5,)),
        ],
        compiler_params=pltpu.CompilerParams(
            collective_id=0, has_side_effects=True, vmem_limit_bytes=62 * 2**20
        ),
    )(
        tokens, pore_mask, solid_embed.reshape(1, 512), fine_query, fine_key, fine_value, fine_out,
        coarse_query, coarse_key, coarse_value, coarse_out, mlp_in, mlp_out,
        block_ones(), query_table(), key_tables(), fine_scale, coarse_scale,
    )


def solution(mesh):
    placed = (P("tile", "region", None), P("tile", "region")) + (P(),) * 13
    return jax.shard_map(
        body, mesh=mesh, in_specs=placed, out_specs=P("tile", "region", None), check_vma=False
    )
```

time: 123 us -> 109 us (0.89)
  Pallas kernels: 117 us -> 105 us
  other arithmetic: 1.92 us -> 0 us
    pallas_call x1, Pallas kernels: 117 us -> 105 us  [body(): pl.pallas_call(layer, out_shape=jax.ShapeDtypeStruct((16, 128, 512), BF16...]
where the time goes in v2:
time: 109 us
  Pallas kernels  105 us (96%)
  local copies, waits for them, and re-layouts  3.1 us (3%)
    pallas_call x1, Pallas kernels, body(): pl.pallas_call(layer, out_shape=jax.ShapeDtypeStruct((16, 128, 512), BF16...  105 us
    unnamed x1, local copies, waits for them, and re-layouts  3.1 us

profile of v2, /device:TPU:0, one launch (start us, length us, event | category | flops | bytes accessed | tf_op | source)
XLA Modules:
  0.0 108.5 jit_solution(12049068340908682215)
XLA Ops:
  0.0 105.4 %shard_map.172 = bf16[16,128,512]{2,1,0:T(8,128)(2,1)} custom-call(bf16[16,128,512]{2,1,0:T(8,128)(2,1)} %tok_ref.1, s32[16,128]{1,0:T(8,128)} %mask_ref.1, f32[1,512]{1,0:T(1,128)} %bitcast.1, bf16[512,512]{1,0:T(8,128)(2,1)} %wq_ref.1, bf16[512,512]{1,0:T(8,128)(2,1)} %wk_ref.1, bf16[512,512]{1,0:T(8,128)(2,1)} %wv_ref.1, bf16[512,512]{1,0:T(8,128)(2,1)} %wo_ref.1, ...), custom_call_target="tpu_custom_call" | custom-call | tf_op jit(solution)/shard_map/pallas_call | solution.py:520
  105.4 3.1 %copy.20 = bf16[16,128,512]{2,1,0:T(8,128)(2,1)} copy(bf16[16,128,512]{2,1,0:T(8,128)(2,1)} %shard_map.172) | data formatting | bytes 4194304

commit v3 on v2

--- a/solution.py
+++ b/solution.py
@@ -31,11 +31,12 @@
 
 
 def gelu(x):
+    x = x.astype(BF16)
     z = jnp.abs(x)
-    p = TAIL[5] * z + TAIL[4]
+    p = z * BF16(TAIL[5]) + BF16(TAIL[4])
     for c in TAIL[3::-1]:
-        p = p * z + c
-    return jnp.maximum(x, 0.0) - z * jnp.exp2(p)
+        p = p * z + BF16(c)
+    return jnp.maximum(x, BF16(0)) - z * jnp.exp2(p)
 
 
 def block_ones():
@@ -154,10 +155,12 @@
     mixed = stream + mm(fine_s[:, at, :].reshape(count, 512), wo) + fb
     nm = normalize(mixed).astype(BF16)
     acc = mixed
+    ahead = mm(nm, w1_s[:, :512])
     for f in range(4):
-        part = slice(512 * f, 512 * f + 512)
-        h = gelu(mm(nm, w1_s[:, part])).astype(BF16)
-        acc = acc + mm(h, w2_s[part, :])
+        now = ahead
+        if f < 3:
+            ahead = mm(nm, w1_s[:, 512 * f + 512 : 512 * f + 1024])
+        acc = acc + mm(gelu(now), w2_s[512 * f : 512 * f + 512, :])
     out_s[:, at, :] = acc.astype(BF16).reshape(16, cols, 512)
 
 
@@ -228,27 +231,23 @@
     dn_buf[:, REST, :] = jnp.zeros((8, 16, 512), BF16)
     load_tok.wait()
 
-    @pl.loop(0, 8)
-    def _(i):
-        pair = []
-        for s in range(2):
-            row = 2 * i + s
+    def norm_rows(i):
+        lo, hi = [], []
+        total = jnp.zeros((128, 512), F32)
+        for k in range(4):
+            row = 4 * i + k
             m = jnp.broadcast_to(mask_ref[pl.ds(row, 1), :].astype(F32), (128, 128)).T.astype(BF16)
             mask_s[row] = m
             n = normalize(stream_of(tok_s[row], m, emb_ref[...]))
             nb = n.astype(BF16)
             buf[row] = nb
-            psum[i // 4] += nb.astype(F32)
-            pair.append(n)
-        at = pl.ds(pl.multiple_of(16 * i, 16), 16)
-        ls_s[at, :] = jnp.concatenate([n[:8] for n in pair], axis=0).astype(BF16)
-        rs_s[at, :] = jnp.concatenate([n[120:] for n in pair], axis=0).astype(BF16)
-
-    cin = normalize(jnp.sum(psum[...].reshape(32, 8, 512), axis=1) * (1.0 / 64.0)).astype(BF16)
-    cin_s[...] = cin
-    x_s[core, g] = cin
-
-    pl.semaphore_wait(barrier, 26)
+            total = total + nb.astype(F32)
+            lo.append(n[:8])
+            hi.append(n[120:])
+        psum[i // 2] += total
+        at = pl.ds(pl.multiple_of(32 * i, 32), 32)
+        ls_s[at, :] = jnp.concatenate(lo, axis=0).astype(BF16)
+        rs_s[at, :] = jnp.concatenate(hi, axis=0).astype(BF16)
 
     sides = [copy(ls_s, rr_s, 0, to_left), copy(rs_s, lr_s, 1, to_right)]
     first, last = pl.ds(0, 64), pl.ds(64, 64)
@@ -267,25 +266,34 @@
             copy(buf.at[pl.ds(9, 7), src, :], up_buf.at[pl.ds(1, 7), dst, :], 10 + k, {"tile": following, "region": r}),
         )
 
+    @pl.loop(0, 2)
+    def _(i):
+        norm_rows(i)
+
+    pl.semaphore_wait(barrier, 26)
+    row_piece(0)[0].start()
+
+    @pl.loop(2, 4)
+    def _(i):
+        norm_rows(i)
+
+    row_piece(0)[1].start()
+    for c in sides:
+        c.start()
+    cin = normalize(jnp.sum(psum[...].reshape(32, 8, 512), axis=1) * (1.0 / 64.0)).astype(BF16)
+    cin_s[...] = cin
+    x_s[core, g] = cin
+
     def gather(step):
         return copy(cin_s, x_s.at[core, g], 13 + step, plane(step))
-
-    for c in sides:
-        c.start()
 
     @pl.loop(1, 16)
     def _(step):
         gather(step).start()
 
+    for c in row_piece(1):
+        c.start()
     for c in corners[:2]:
-        c.start()
-
-    @pl.loop(0, 4)
-    def _(k):
-        for c in row_piece(k):
-            c.start()
-
-    for c in corners[2:]:
         c.start()
 
     loads[CQUERY].wait()
@@ -330,9 +338,9 @@
         replies.append(copy(po_s.at[rows, :], rz_s.at[z], 32 + step, column(step)))
         replies.append(copy(ps_s.at[:, rows, :], rst_s.at[z], 35 + step, column(step)))
 
-    @pl.loop(0, 8)
+    @pl.loop(0, 4)
     def _(j):
-        @pl.when(j == 3)
+        @pl.when(j == 2)
         def _():
             sibling.wait_recv()
             for c in asks:
@@ -346,9 +354,13 @@
             rz_s[z] = po_s[mine, :]
             rst_s[z] = ps_s[:, mine, :]
 
-        for p in range(4):
-            attend_own(j, p, q_s, k_s, v_s, qt_ref, kt_ref, c_ref, o_s, l_s, m_s)
-
+        for p in range(8):
+            attend_own(2 * j + p // 4, p % 4, q_s, k_s, v_s, qt_ref, kt_ref, c_ref, o_s, l_s, m_s)
+
+    for c in row_piece(0):
+        c.wait_send()
+    for c in row_piece(2):
+        c.start()
     for c in replies:
         c.wait_recv()
     loads[COUT].wait()
@@ -409,24 +421,27 @@
         ku_s[:, cols, :], kd_s[:, cols, :] = keys[:8], keys[8:]
         vu_s[:, cols, :], vd_s[:, cols, :] = vals[:8], vals[8:]
 
-        @pl.when(i > 0)
+        @pl.when(i == 0)
+        def _():
+            attend(0)
+            close(0, 16, 0)
+
+        @pl.when(i == 1)
+        def _():
+            for c in row_piece(1):
+                c.wait_send()
+            for c in row_piece(3) + tuple(corners[2:]):
+                c.start()
+
+        @pl.when((i > 0) & (i < 4))
         def _():
             attend(2 * i - 1)
-
-        @pl.when(i < 4)
-        def _():
             attend(2 * i)
-
-        @pl.when(i == 0)
-        def _():
-            close(0, 16, 0)
-
-        @pl.when((i > 0) & (i < 4))
-        def _():
             close(32 * i - 16, 32, i)
 
         @pl.when(i == 4)
         def _():
+            attend(7)
             close(112, 16, 4)
 
     store(0, 16, 0).wait()
@@ -439,8 +454,7 @@
     for c in sides + corners + asks + [sibling] + replies:
         c.wait_send()
 
-    @pl.loop(0, 4)
-    def _(k):
+    for k in (2, 3):
         for c in row_piece(k):
             c.wait_send()
 

time: 109 us -> 85.3 us (0.78)
  the two profiles are of different devices: /device:TPU:0 before, /device:TPU:33 now
where the time goes in v3:
time: 85.3 us; the launch traced here: 85.1 us
  Pallas kernels  82 us (96%)
  local copies, waits for them, and re-layouts  3.1 us (4%)
    pallas_call x1, Pallas kernels, body(): pl.pallas_call(layer, out_shape=jax.ShapeDtypeStruct((16, 128, 512), BF16...  82 us
    unnamed x1, local copies, waits for them, and re-layouts  3.1 us

profile of v3, /device:TPU:33, one launch (start us, length us, event | category | flops | bytes accessed | tf_op | source)
XLA Modules:
  0.0 85.1 jit_solution(10907134326916675618)
XLA Ops:
  0.0 82.0 %shard_map.172 = bf16[16,128,512]{2,1,0:T(8,128)(2,1)} custom-call(bf16[16,128,512]{2,1,0:T(8,128)(2,1)} %tok_ref.1, s32[16,128]{1,0:T(8,128)} %mask_ref.1, f32[1,512]{1,0:T(1,128)} %bitcast.1, bf16[512,512]{1,0:T(8,128)(2,1)} %wq_ref.1, bf16[512,512]{1,0:T(8,128)(2,1)} %wk_ref.1, bf16[512,512]{1,0:T(8,128)(2,1)} %wv_ref.1, bf16[512,512]{1,0:T(8,128)(2,1)} %wo_ref.1, ...), custom_call_target="tpu_custom_call" | custom-call | tf_op jit(solution)/shard_map/pallas_call | solution.py:534
  82.0 3.1 %copy.20 = bf16[16,128,512]{2,1,0:T(8,128)(2,1)} copy(bf16[16,128,512]{2,1,0:T(8,128)(2,1)} %shard_map.172) | data formatting | bytes 4194304

commit v4 on v3

--- a/solution.py
+++ b/solution.py
@@ -197,6 +197,18 @@
             device_id=where, device_id_type=MESH,
         )
 
+    barrier = pltpu.get_barrier_semaphore()
+    to_left, to_right = {"tile": t, "region": left}, {"tile": t, "region": right}
+    for where in [to_left, to_right] + [{"tile": a, "region": b} for a in (prev, following) for b in (left, r, right)]:
+        pl.semaphore_signal(barrier, inc=1, device_id=where, device_id_type=MESH)
+
+    @pl.loop(1, 16)
+    def _(step):
+        pl.semaphore_signal(barrier, inc=1, device_id=plane(step), device_id_type=MESH)
+
+    for step in (1, 2, 3):
+        pl.semaphore_signal(barrier, inc=1, device_id=column(step), device_id_type=MESH)
+
     load_tok = pltpu.make_async_copy(tok_ref, tok_s, load_sem.at[0])
     load_tok.start()
     names = (wq_ref, wk_ref, wv_ref, wo_ref, cwq_ref, cwk_ref, cwv_ref, cwo_ref)
@@ -207,18 +219,6 @@
         loads[i].start()
     load_1.start()
     load_2.start()
-
-    barrier = pltpu.get_barrier_semaphore()
-    to_left, to_right = {"tile": t, "region": left}, {"tile": t, "region": right}
-    for where in [to_left, to_right] + [{"tile": a, "region": b} for a in (prev, following) for b in (left, r, right)]:
-        pl.semaphore_signal(barrier, inc=1, device_id=where, device_id_type=MESH)
-
-    @pl.loop(1, 16)
-    def _(step):
-        pl.semaphore_signal(barrier, inc=1, device_id=plane(step), device_id_type=MESH)
-
-    for step in (1, 2, 3):
-        pl.semaphore_signal(barrier, inc=1, device_id=column(step), device_id_type=MESH)
 
     ones = ones_ref[...]
     for h in range(HEADS):
@@ -266,65 +266,72 @@
             copy(buf.at[pl.ds(9, 7), src, :], up_buf.at[pl.ds(1, 7), dst, :], 10 + k, {"tile": following, "region": r}),
         )
 
-    @pl.loop(0, 2)
+    @pl.loop(0, 4)
     def _(i):
         norm_rows(i)
 
-    pl.semaphore_wait(barrier, 26)
-    row_piece(0)[0].start()
-
-    @pl.loop(2, 4)
-    def _(i):
-        norm_rows(i)
-
-    row_piece(0)[1].start()
-    for c in sides:
-        c.start()
     cin = normalize(jnp.sum(psum[...].reshape(32, 8, 512), axis=1) * (1.0 / 64.0)).astype(BF16)
     cin_s[...] = cin
     x_s[core, g] = cin
+    loads[CQUERY].wait()
+    cq = head_norm(mm(cin, w_s[CQUERY]), ones)
+    cq_s[...] = cq
+    qz_s[z] = cq
+    loads[QUERY].wait()
+
+    @pl.loop(0, 4)
+    def _(i):
+        rows = pl.ds(4 * i, 4)
+        q_s[rows] = head_norm(mm(buf[rows].reshape(512, 512), w_s[QUERY]), ones).reshape(4, 128, 512)
+
+    loads[KEY].wait()
+    loads[VALUE].wait()
+
+    def own_keys(i):
+        rows = pl.ds(4 * i, 4)
+        side = jnp.zeros((4, 8, 512), F32)
+        n = jnp.concatenate([side, buf[rows].astype(F32), side], axis=1).astype(BF16)
+        keys, vals = project(n.reshape(576, 512), w_s[KEY], w_s[VALUE], ones)
+        k_s[rows] = keys.reshape(4, 144, 512)
+        v_s[rows] = vals.reshape(4, 144, 512)
+
+    @pl.loop(0, 2)
+    def _(i):
+        own_keys(i)
 
     def gather(step):
         return copy(cin_s, x_s.at[core, g], 13 + step, plane(step))
+
+    asks = [copy(cq_s, qz_s.at[z], 28 + step, column(step)) for step in (1, 2, 3)]
+    pl.semaphore_wait(barrier, 26)
+    for c in sides:
+        c.start()
 
     @pl.loop(1, 16)
     def _(step):
         gather(step).start()
+
+    for c in asks:
+        c.start()
+    for c in row_piece(0):
+        c.start()
+
+    @pl.loop(2, 4)
+    def _(i):
+        own_keys(i)
+
+    def attend_pair(first, second):
+        for p in range(8):
+            attend_own((first, second)[p // 4], p % 4, q_s, k_s, v_s, qt_ref, kt_ref, c_ref, o_s, l_s, m_s)
+
+    @pl.loop(0, 3)
+    def _(j):
+        attend_pair(2 * j + 1, 2 * j + 2)
 
     for c in row_piece(1):
         c.start()
     for c in corners[:2]:
         c.start()
-
-    loads[CQUERY].wait()
-    cq = head_norm(mm(cin, w_s[CQUERY]), ones)
-    cq_s[...] = cq
-    qz_s[z] = cq
-    asks = [copy(cq_s, qz_s.at[z], 28 + step, column(step)) for step in (1, 2, 3)]
-    for c in asks:
-        c.start()
-
-    loads[QUERY].wait()
-
-    @pl.loop(0, 4)
-    def _(i):
-        rows = pl.ds(4 * i, 4)
-        q_s[rows] = head_norm(mm(buf[rows].reshape(512, 512), w_s[QUERY]), ones).reshape(4, 128, 512)
-
-    loads[KEY].wait()
-    loads[VALUE].wait()
-    for c in sides:
-        c.wait_recv()
-
-    @pl.loop(0, 4)
-    def _(i):
-        rows = pl.ds(4 * i, 4)
-        at = pl.ds(pl.multiple_of(32 * i, 32), 32)
-        near = [ref[at, :].astype(F32).reshape(4, 8, 512) for ref in (lr_s, rr_s)]
-        n = jnp.concatenate([near[0], buf[rows].astype(F32), near[1]], axis=1).astype(BF16)
-        keys, vals = project(n.reshape(576, 512), w_s[KEY], w_s[VALUE], ones)
-        k_s[rows] = keys.reshape(4, 144, 512)
-        v_s[rows] = vals.reshape(4, 144, 512)
 
     @pl.loop(1, 16)
     def _(step):
@@ -338,37 +345,37 @@
         replies.append(copy(po_s.at[rows, :], rz_s.at[z], 32 + step, column(step)))
         replies.append(copy(ps_s.at[:, rows, :], rst_s.at[z], 35 + step, column(step)))
 
-    @pl.loop(0, 4)
-    def _(j):
-        @pl.when(j == 2)
-        def _():
-            sibling.wait_recv()
-            for c in asks:
-                c.wait_recv()
-            loads[CKEY].wait()
-            loads[CVALUE].wait()
-            coarse_part(x_s, qz_s, w_s, cc_ref, ones, ck_s, cv_s, po_s, ps_s)
-            for c in replies:
-                c.start()
-            mine = pl.ds(pl.multiple_of(32 * z, 32), 32)
-            rz_s[z] = po_s[mine, :]
-            rst_s[z] = ps_s[:, mine, :]
-
-        for p in range(8):
-            attend_own(2 * j + p // 4, p % 4, q_s, k_s, v_s, qt_ref, kt_ref, c_ref, o_s, l_s, m_s)
-
+    for c in sides:
+        c.wait_recv()
+    edges = [
+        lr_s[...].astype(F32).reshape(16, 8, 512),
+        buf[:, 0:16, :].astype(F32)[:, :8],
+        buf[:, 112:128, :].astype(F32)[:, 8:],
+        rr_s[...].astype(F32).reshape(16, 8, 512),
+    ]
+    n = [jnp.concatenate(edges[i : i + 2], axis=1).astype(BF16).reshape(256, 512) for i in (0, 2)]
+    keys, vals = project(jnp.concatenate(n, axis=0), w_s[KEY], w_s[VALUE], ones)
+    for i, cols in ((0, pl.ds(0, 16)), (1, pl.ds(128, 16))):
+        part = slice(256 * i, 256 * i + 256)
+        k_s[:, cols, :] = keys[part].reshape(16, 16, 512)
+        v_s[:, cols, :] = vals[part].reshape(16, 16, 512)
+    attend_pair(0, 7)
+
+    sibling.wait_recv()
+    for c in asks:
+        c.wait_recv()
+    loads[CKEY].wait()
+    loads[CVALUE].wait()
+    coarse_part(x_s, qz_s, w_s, cc_ref, ones, ck_s, cv_s, po_s, ps_s)
+    for c in replies:
+        c.start()
+    mine = pl.ds(pl.multiple_of(32 * z, 32), 32)
+    rz_s[z] = po_s[mine, :]
+    rst_s[z] = ps_s[:, mine, :]
     for c in row_piece(0):
         c.wait_send()
     for c in row_piece(2):
         c.start()
-    for c in replies:
-        c.wait_recv()
-    loads[COUT].wait()
-    feedback = mm(coarse_join(rz_s, rst_s), w_s[COUT])
-    fb_s[...] = jnp.broadcast_to(feedback.reshape(32, 1, 512), (32, 8, 512)).reshape(2, 16, 8, 512)
-    loads[OUT].wait()
-    load_1.wait()
-    load_2.wait()
 
     def place(source, dst, where):
         x = source.astype(F32).reshape(8, 8, 512)
@@ -424,6 +431,14 @@
         @pl.when(i == 0)
         def _():
             attend(0)
+            for c in replies:
+                c.wait_recv()
+            loads[COUT].wait()
+            feedback = mm(coarse_join(rz_s, rst_s), w_s[COUT])
+            fb_s[...] = jnp.broadcast_to(feedback.reshape(32, 1, 512), (32, 8, 512)).reshape(2, 16, 8, 512)
+            loads[OUT].wait()
+            load_1.wait()
+            load_2.wait()
             close(0, 16, 0)
 
         @pl.when(i == 1)

time: 85.3 us -> 78.6 us (0.921)
  the two profiles are of different devices: /device:TPU:33 before, /device:TPU:0 now
where the time goes in v4:
time: 78.6 us; the launch traced here: 77.7 us
  Pallas kernels  74.6 us (95%)
  local copies, waits for them, and re-layouts  3.1 us (4%)
    pallas_call x1, Pallas kernels, body(): pl.pallas_call(layer, out_shape=jax.ShapeDtypeStruct((16, 128, 512), BF16...  74.6 us
    unnamed x1, local copies, waits for them, and re-layouts  3.1 us

profile of v4, /device:TPU:0, one launch (start us, length us, event | category | flops | bytes accessed | tf_op | source)
XLA Modules:
  0.0 77.7 jit_solution(1408759050219709754)
XLA Ops:
  0.0 74.6 %shard_map.172 = bf16[16,128,512]{2,1,0:T(8,128)(2,1)} custom-call(bf16[16,128,512]{2,1,0:T(8,128)(2,1)} %tok_ref.1, s32[16,128]{1,0:T(8,128)} %mask_ref.1, f32[1,512]{1,0:T(1,128)} %bitcast.1, bf16[512,512]{1,0:T(8,128)(2,1)} %wq_ref.1, bf16[512,512]{1,0:T(8,128)(2,1)} %wk_ref.1, bf16[512,512]{1,0:T(8,128)(2,1)} %wv_ref.1, bf16[512,512]{1,0:T(8,128)(2,1)} %wo_ref.1, ...), custom_call_target="tpu_custom_call" | custom-call | tf_op jit(solution)/shard_map/pallas_call | solution.py:549
  74.6 3.1 %copy.20 = bf16[16,128,512]{2,1,0:T(8,128)(2,1)} copy(bf16[16,128,512]{2,1,0:T(8,128)(2,1)} %shard_map.172) | data formatting | bytes 4194304

commit v5 on v4

--- a/solution.py
+++ b/solution.py
@@ -258,13 +258,19 @@
         copy(ls_s.at[last, :], corner_s.at[3], 5, {"tile": following, "region": left}),
     ]
 
+    def row_part(start, cols, up, down):
+        src = pl.ds(pl.multiple_of(start, 16), cols)
+        dst = pl.ds(pl.multiple_of(16 + start, 16), cols)
+        return (
+            copy(buf.at[pl.ds(0, 7), src, :], dn_buf.at[pl.ds(0, 7), dst, :], up, {"tile": prev, "region": r}),
+            copy(buf.at[pl.ds(9, 7), src, :], up_buf.at[pl.ds(1, 7), dst, :], down, {"tile": following, "region": r}),
+        )
+
     def row_piece(k):
-        src = pl.ds(pl.multiple_of(32 * k, 16), 32)
-        dst = pl.ds(pl.multiple_of(16 + 32 * k, 16), 32)
-        return (
-            copy(buf.at[pl.ds(0, 7), src, :], dn_buf.at[pl.ds(0, 7), dst, :], 6 + k, {"tile": prev, "region": r}),
-            copy(buf.at[pl.ds(9, 7), src, :], up_buf.at[pl.ds(1, 7), dst, :], 10 + k, {"tile": following, "region": r}),
-        )
+        return row_part(32 * k, 32, 6 + k, 10 + k)
+
+    late = row_part(96, 16, 9, 13)
+    latest = row_part(112, 16, 39, 40)
 
     @pl.loop(0, 4)
     def _(i):
@@ -343,7 +349,7 @@
     for step in (1, 2, 3):
         rows = pl.ds(pl.multiple_of(32 * ((z + step) % 4), 32), 32)
         replies.append(copy(po_s.at[rows, :], rz_s.at[z], 32 + step, column(step)))
-        replies.append(copy(ps_s.at[:, rows, :], rst_s.at[z], 35 + step, column(step)))
+        replies.append(copy(ps_s.at[rows, :], rst_s.at[z], 35 + step, column(step)))
 
     for c in sides:
         c.wait_recv()
@@ -371,7 +377,7 @@
         c.start()
     mine = pl.ds(pl.multiple_of(32 * z, 32), 32)
     rz_s[z] = po_s[mine, :]
-    rst_s[z] = ps_s[:, mine, :]
+    rst_s[z] = ps_s[mine, :]
     for c in row_piece(0):
         c.wait_send()
     for c in row_piece(2):
@@ -399,12 +405,20 @@
         finish(start, cols, fine_s, tok_s, mask_s, emb_ref, fb_s, w_s[OUT], w1_s, w2_s, out_s)
         store(start, cols, index).start()
 
-    @pl.loop(0, 5)
+    def halo(start, width):
+        src = pl.ds(pl.multiple_of(start, 16), width + 16)
+        cols = pl.ds(pl.multiple_of(start, 16), width)
+        n = [b[:, src, :].astype(F32)[:, 8 : width + 8].astype(BF16) for b in (up_buf, dn_buf)]
+        n = jnp.concatenate(n, axis=0).reshape(16 * width, 512)
+        keys, vals = project(n, w_s[KEY], w_s[VALUE], ones)
+        keys, vals = keys.reshape(16, width, 512), vals.reshape(16, width, 512)
+        ku_s[:, cols, :], kd_s[:, cols, :] = keys[:8], keys[8:]
+        vu_s[:, cols, :], vd_s[:, cols, :] = vals[:8], vals[8:]
+
+    @pl.loop(0, 3)
     def _(i):
-        @pl.when(i < 4)
-        def _():
-            for c in row_piece(i):
-                c.wait_recv()
+        for c in row_piece(i):
+            c.wait_recv()
 
         @pl.when(i == 0)
         def _():
@@ -413,20 +427,7 @@
             place(corner_s[0], dn_buf, LEFT)
             place(corner_s[1], up_buf, LEFT)
 
-        @pl.when(i == 4)
-        def _():
-            for c in corners[2:]:
-                c.wait_recv()
-            place(corner_s[2], dn_buf, RIGHT)
-            place(corner_s[3], up_buf, RIGHT)
-
-        src = pl.ds(pl.multiple_of(32 * i, 32), 48)
-        cols = pl.ds(pl.multiple_of(32 * i, 32), 32)
-        n = jnp.concatenate([b[:, src, :].astype(F32)[:, 8:40].astype(BF16) for b in (up_buf, dn_buf)], axis=0)
-        keys, vals = project(n.reshape(512, 512), w_s[KEY], w_s[VALUE], ones)
-        keys, vals = keys.reshape(16, 32, 512), vals.reshape(16, 32, 512)
-        ku_s[:, cols, :], kd_s[:, cols, :] = keys[:8], keys[8:]
-        vu_s[:, cols, :], vd_s[:, cols, :] = vals[:8], vals[8:]
+        halo(32 * i, 32)
 
         @pl.when(i == 0)
         def _():
@@ -445,33 +446,40 @@
         def _():
             for c in row_piece(1):
                 c.wait_send()
-            for c in row_piece(3) + tuple(corners[2:]):
+            for c in late + tuple(corners[2:]) + latest:
                 c.start()
 
-        @pl.when((i > 0) & (i < 4))
+        @pl.when(i > 0)
         def _():
             attend(2 * i - 1)
             attend(2 * i)
             close(32 * i - 16, 32, i)
 
-        @pl.when(i == 4)
-        def _():
-            attend(7)
-            close(112, 16, 4)
+    for c in late:
+        c.wait_recv()
+    halo(96, 16)
+    attend(5)
+    close(80, 16, 3)
+    for c in latest + tuple(corners[2:]):
+        c.wait_recv()
+    place(corner_s[2], dn_buf, RIGHT)
+    place(corner_s[3], up_buf, RIGHT)
+    halo(112, 32)
+    attend(6)
+    attend(7)
+    close(96, 32, 4)
 
     store(0, 16, 0).wait()
 
-    @pl.loop(1, 4)
-    def _(i):
-        store(32 * i - 16, 32, i).wait()
-
-    store(112, 16, 4).wait()
+    store(16, 32, 1).wait()
+    store(48, 32, 2).wait()
+    store(80, 16, 3).wait()
+    store(96, 32, 4).wait()
     for c in sides + corners + asks + [sibling] + replies:
         c.wait_send()
 
-    for k in (2, 3):
-        for c in row_piece(k):
-            c.wait_send()
+    for c in row_piece(2) + late + latest:
+        c.wait_send()
 
     @pl.loop(1, 16)
     def _(step):
@@ -491,34 +499,33 @@
     lane = lax.broadcasted_iota(jnp.int32, (128, 128), 1)
     head = lax.broadcasted_iota(jnp.int32, (128, 256), 1) // 64
     tops = jnp.zeros((128, 128), F32)
-    sums = jnp.zeros((128, 128), F32)
     for half in range(2):
         lanes = slice(256 * half, 256 * half + 256)
         qh = q[:, lanes]
         rows = jnp.concatenate([jnp.where(head == h, qh, jnp.zeros_like(qh)) for h in range(4)], axis=0)
         s = lax.dot_general(rows, ck_s[:, lanes], NT, preferred_element_type=F32)
-        weights = []
+        weights, totals = [], []
         for h in range(4):
             c = cc_ref[4 * half + h]
             part = s[128 * h : 128 * h + 128]
             top = jnp.max(part, axis=-1, keepdims=True)
             w = jnp.exp2((part - top) * c)
-            tops = jnp.where(lane == 4 * half + h, top * c, tops)
-            sums = jnp.where(lane == 4 * half + h, jnp.sum(w, axis=-1, keepdims=True), sums)
+            total = jnp.sum(w, axis=-1, keepdims=True)
+            tops = jnp.where(lane == 4 * half + h, top * c + jnp.log2(total), tops)
+            totals.append(total)
             weights.append(w.astype(BF16))
         o = mm(jnp.concatenate(weights, axis=0), cv_s[:, lanes])
-        picked = o[:128]
+        picked = o[:128] / totals[0]
         for h in range(1, 4):
-            picked = jnp.where(head == h, o[128 * h : 128 * h + 128], picked)
-        po_s[:, lanes] = picked
-    ps_s[0] = tops
-    ps_s[1] = sums
+            picked = jnp.where(head == h, o[128 * h : 128 * h + 128] / totals[h], picked)
+        po_s[:, lanes] = picked.astype(BF16)
+    ps_s[...] = tops
 
 
 def coarse_join(rz_s, rs_s):
-    top = jnp.maximum(jnp.maximum(rs_s[0, 0], rs_s[1, 0]), jnp.maximum(rs_s[2, 0], rs_s[3, 0]))
-    scale = [jnp.exp2(rs_s[i, 0] - top) for i in range(4)]
-    total = sum(scale[i] * rs_s[i, 1] for i in range(4))
+    top = jnp.maximum(jnp.maximum(rs_s[0], rs_s[1]), jnp.maximum(rs_s[2], rs_s[3]))
+    scale = [jnp.exp2(rs_s[i] - top) for i in range(4)]
+    total = sum(scale)
     low = lax.broadcasted_iota(jnp.int32, (32, 128), 1) < 64
     joined = jnp.zeros((32, 512), F32)
     for i in range(4):
@@ -527,7 +534,7 @@
             jnp.where(low, jnp.broadcast_to(a[:, 2 * p : 2 * p + 1], (32, 128)), jnp.broadcast_to(a[:, 2 * p + 1 : 2 * p + 2], (32, 128)))
             for p in range(4)
         ]
-        joined = joined + jnp.concatenate(wide, axis=1) * rz_s[i]
+        joined = joined + jnp.concatenate(wide, axis=1) * rz_s[i].astype(F32)
     return joined.astype(BF16)
 
 
@@ -584,10 +591,10 @@
             half(1024, 512),
             half(1024, 512),
             half(4, 32, 512),
-            full(128, 512),
-            full(2, 128, 128),
-            full(4, 32, 512),
-            full(4, 2, 32, 128),
+            half(128, 512),
+            full(128, 128),
+            half(4, 32, 512),
+            full(4, 32, 128),
             full(2, 16, 8, 512),
             pltpu.SMEM((8,), F32),
             pltpu.SMEM((8,), F32),

time: 78.6 us -> 74.8 us (0.952)
  Pallas kernels: 74.6 us -> 71.6 us
    pallas_call x1, Pallas kernels: 74.6 us -> 71.6 us  [body(): pl.pallas_call(layer, out_shape=jax.ShapeDtypeStruct((16, 128, 512), BF16...]
where the time goes in v5:
time: 74.8 us; the launch traced here: 74.7 us
  Pallas kernels  71.6 us (96%)
  local copies, waits for them, and re-layouts  3.1 us (4%)
    pallas_call x1, Pallas kernels, body(): pl.pallas_call(layer, out_shape=jax.ShapeDtypeStruct((16, 128, 512), BF16...  71.6 us
    unnamed x1, local copies, waits for them, and re-layouts  3.1 us

profile of v5, /device:TPU:0, one launch (start us, length us, event | category | flops | bytes accessed | tf_op | source)
XLA Modules:
  0.0 74.7 jit_solution(16678000525555273454)
XLA Ops:
  0.0 71.6 %shard_map.172 = bf16[16,128,512]{2,1,0:T(8,128)(2,1)} custom-call(bf16[16,128,512]{2,1,0:T(8,128)(2,1)} %tok_ref.1, s32[16,128]{1,0:T(8,128)} %mask_ref.1, f32[1,512]{1,0:T(1,128)} %bitcast.1, bf16[512,512]{1,0:T(8,128)(2,1)} %wq_ref.1, bf16[512,512]{1,0:T(8,128)(2,1)} %wk_ref.1, bf16[512,512]{1,0:T(8,128)(2,1)} %wv_ref.1, bf16[512,512]{1,0:T(8,128)(2,1)} %wo_ref.1, ...), custom_call_target="tpu_custom_call" | custom-call | tf_op jit(solution)/shard_map/pallas_call | solution.py:556
  71.6 3.1 %copy.20 = bf16[16,128,512]{2,1,0:T(8,128)(2,1)} copy(bf16[16,128,512]{2,1,0:T(8,128)(2,1)} %shard_map.172) | data formatting | bytes 4194304
